TPU v7x, 256 devices: a whole 4x4x8 slice. The times are simulated.
256 devices in a mesh: rows: 4 (over x), chan: 8 (over y, z_lo), filt: 8 (over z_hi, core).
Axes of the slice: x: 4, y: 4, z: 8 (z_hi: 4, z_lo: 2; z = z_hi * 2 + z_lo), core: 2. Of those that a mesh axis runs over, the one named last changes fastest.
Arguments:
- images: bfloat16 [16, 2048, 2048], P('rows', 'chan', 'filt'), may hold values from -6 to 6
- first_weight: bfloat16 [2048, 1024], P('chan', 'filt'), may hold values from -0.125 to 0.125
- group_weight: bfloat16 [3, 3, 32, 1024], P(None, None, None, 'filt'), may hold values from -0.375 to 0.375
- third_weight: bfloat16 [1024, 2048], P('chan', 'filt'), may hold values from -0.1875 to 0.1875
- out_grad: bfloat16 [16, 2048, 2048], P('rows', 'chan', 'filt'), may hold values from -6 to 6
Outputs:
- block_out: bfloat16 [16, 2048, 2048], P('rows', 'chan', 'filt')
- images_grad: float32 [16, 2048, 2048], P('rows', 'chan', 'filt')
- first_grad: float32 [2048, 1024], P('chan', 'filt')
- group_grad: float32 [3, 3, 32, 1024], P(None, None, None, 'filt')
- third_grad: float32 [1024, 2048], P('chan', 'filt')
All inputs are finite; a program needn't handle non-finite values.
Results may differ from a plain program's by a relative error of at most 0.006.
Values may be sent and summed in bfloat16 or wider, within the bound.
No kernel may reach another device: no remote copies, remote signals or barrier semaphores. Data moves between devices by JAX's collectives and lax.ppermute only.
A program may use at most 128 MiB of HBM per device.

v0:
```python
import jax
import jax.numpy as jnp
from jax import lax
from jax.sharding import PartitionSpec as P


def extended(block, sides, width):
    for axis, dim in sides:
        count = lax.axis_size(axis)
        forward = [(i, i + 1) for i in range(count - 1)]
        backward = [(target, source) for source, target in forward]
        low = lax.ppermute(
            lax.slice_in_dim(block, block.shape[dim] - width, None, axis=dim), axis, forward
        )
        high = lax.ppermute(lax.slice_in_dim(block, 0, width, axis=dim), axis, backward)
        block = jnp.concatenate([low, block, high], axis=dim)
    return block


def silu_slope(values):
    logistic = jax.nn.sigmoid(values)
    return logistic * (1.0 + values * (1.0 - logistic))


def group_conv(padded, kernel, groups_here):
    result = lax.conv_general_dilated(
        padded[None],
        kernel,
        (1, 1),
        "VALID",
        dimension_numbers=("NHWC", "HWIO", "NHWC"),
        feature_group_count=groups_here,
        preferred_element_type=jnp.float32,
    )
    return result[0]


def transposed_kernel(kernel, group_size, groups_here):
    pieces = kernel.reshape(3, 3, group_size, groups_here, group_size)
    swapped = jnp.transpose(pieces, (0, 1, 4, 3, 2)).reshape(
        3, 3, group_size, groups_here * group_size
    )
    return swapped[::-1, ::-1]


def kernel_partial(padded_first, group_delta, group_size, groups_here):
    rows_here = group_delta.shape[0]
    cols_here = group_delta.shape[1]
    pixels = rows_here * cols_here
    delta_groups = group_delta.reshape(pixels, groups_here, group_size)
    kernel_terms = []
    for row_shift in range(3):
        for col_shift in range(3):
            window = padded_first[
                row_shift : row_shift + rows_here, col_shift : col_shift + cols_here
            ]
            window = window.reshape(pixels, groups_here, group_size)
            kernel_terms.append(
                jnp.einsum("pgi,pgo->gio", window, delta_groups, preferred_element_type=jnp.float32)
            )
    kernel_part = jnp.stack(kernel_terms).reshape(3, 3, groups_here, group_size, group_size)
    kernel_part = jnp.transpose(kernel_part, (0, 1, 3, 2, 4))
    return kernel_part.reshape(3, 3, group_size, groups_here * group_size)


def body(images, first_weight, group_weight, third_weight, out_grad):
    rows_here = images.shape[0]
    cols_here = images.shape[1]
    group_size = group_weight.shape[2]
    first_panel, third_panel = (
        lax.all_gather(first_weight, "chan", axis=0, tiled=True),
        lax.all_gather(third_weight, "chan", axis=0, tiled=True),
    )
    pixels = rows_here * cols_here
    groups_here = group_weight.shape[3] // group_size
    gathered = lax.all_gather(images, "filt", axis=2, tiled=True)
    flat_images = gathered.reshape(pixels, gathered.shape[2])
    pre_first = jnp.dot(flat_images, first_panel, preferred_element_type=jnp.float32)
    act_first = (
        jax.nn.silu(pre_first)
        .astype(jnp.bfloat16)
        .reshape(rows_here, cols_here, first_panel.shape[1])
    )
    padded_first = extended(act_first, (("rows", 0), ("chan", 1)), 1)
    pre_group = group_conv(padded_first, group_weight, groups_here)
    act_group = jax.nn.silu(pre_group).astype(jnp.bfloat16)
    mid_whole = lax.all_gather(act_group, "filt", axis=2, tiled=True)
    flat_mid = mid_whole.reshape(pixels, mid_whole.shape[2])
    third_out = jnp.dot(flat_mid, third_panel, preferred_element_type=jnp.float32)
    own_images = images.reshape(pixels, images.shape[2]).astype(jnp.float32)
    block_out = (own_images + third_out).astype(jnp.bfloat16).reshape(images.shape)
    grad_flat = out_grad.reshape(pixels, out_grad.shape[2])
    mid_terms = lax.dot_general(
        grad_flat, third_panel, (((1,), (1,)), ((), ())), preferred_element_type=jnp.float32
    )
    mid_grad = lax.psum_scatter(
        mid_terms.reshape(rows_here, cols_here, mid_terms.shape[1]),
        "filt",
        scatter_dimension=2,
        tiled=True,
    )
    third_part = lax.dot_general(
        flat_mid, grad_flat, (((0,), (0,)), ((), ())), preferred_element_type=jnp.float32
    )
    group_delta = (mid_grad * silu_slope(pre_group)).astype(jnp.bfloat16)
    padded_delta = extended(group_delta, (("rows", 0), ("chan", 1)), 1)
    first_back = group_conv(
        padded_delta, transposed_kernel(group_weight, group_size, groups_here), groups_here
    )
    kernel_part = kernel_partial(padded_first, group_delta, group_size, groups_here)
    first_delta = (first_back.reshape(pixels, first_back.shape[2]) * silu_slope(pre_first)).astype(
        jnp.bfloat16
    )
    first_part = lax.dot_general(
        flat_images, first_delta, (((0,), (0,)), ((), ())), preferred_element_type=jnp.float32
    )
    input_terms = lax.dot_general(
        first_delta, first_panel, (((1,), (1,)), ((), ())), preferred_element_type=jnp.float32
    )
    back_images = lax.psum_scatter(
        input_terms.reshape(rows_here, cols_here, input_terms.shape[1]).astype(jnp.bfloat16),
        "filt",
        scatter_dimension=2,
        tiled=True,
    ).astype(jnp.float32)
    images_grad = out_grad.astype(jnp.float32) + back_images
    group_grad = lax.psum(kernel_part, ("rows", "chan"))
    first_total, third_total = lax.psum((first_part, third_part), "rows")
    first_grad, third_grad = (
        lax.psum_scatter(first_total, "chan", scatter_dimension=0, tiled=True),
        lax.psum_scatter(third_total, "chan", scatter_dimension=0, tiled=True),
    )
    return (block_out, images_grad, first_grad, group_grad, third_grad)


def solution(mesh):
    in_specs = (
        P("rows", "chan", "filt"),
        P("chan", "filt"),
        P(None, None, None, "filt"),
        P("chan", "filt"),
        P("rows", "chan", "filt"),
    )
    out_specs = (
        P("rows", "chan", "filt"),
        P("rows", "chan", "filt"),
        P("chan", "filt"),
        P(None, None, None, "filt"),
        P("chan", "filt"),
    )
    return jax.shard_map(body, mesh=mesh, in_specs=in_specs, out_specs=out_specs, check_vma=False)
```

profile of v0, /device:TPU:32, one launch (start us, length us, event | category | flops | bytes accessed | tf_op | source)
XLA Modules:
  0.0 700.0 jit_solution(2654013649618200023)
XLA Ops:
  7.9 39.6 %all_gather.15 = bf16[1024,256]{1,0:T(8,128)(2,1)S(1)} all-gather(bf16[128,256]{1,0:T(8,128)(2,1)} %param.8), channel_id=1, replica_groups=mesh['rows'=4,'chan'=8,'filt'=8] {'chan'}, dimensions={0}, use_global_device_ids=true | all-gather | bytes 589824 | tf_op jit(solution)/shard_map/all_gather | solution.py:72
  47.5 3.8 fusion.10
  52.2 36.9 %all_gather.13 = bf16[2048,128]{1,0:T(8,128)(2,1)S(1)} all-gather(bf16[256,128]{1,0:T(8,128)(2,1)S(1)} %copy-done.13), channel_id=1, replica_groups=mesh['rows'=4,'chan'=8,'filt'=8] {'chan'}, dimensions={0}, use_global_device_ids=true | all-gather | bytes 589824 | tf_op jit(solution)/shard_map/all_gather | solution.py:71
  89.1 4.4 multiply_convert_fusion.3
  98.4 4.2 collective-permute-done.1
  103.2 3.4 collective-permute-start.2
  110.7 8.0 %collective-permute-done.2 = bf16[6,1,128]{1,2,0:T(8,128)(2,1)S(1)} collective-permute-done((bf16[6,1,128]{1,2,0:T(8,128)(2,1)S(1)}, bf16[6,1,128]{1,2,0:T(8,128)(2,1)S(1)}, u32[]{:S(2)}, u32[]{:S(2)}) %collective-permute-start.2) | collective-permute-done | bytes 1568 | tf_op jit(solution)/shard_map/ppermute | solution.py:12
  118.7 10.6 %collective-permute-done.3 = bf16[6,1,128]{1,2,0:T(8,128)(2,1)S(1)} collective-permute-done((bf16[6,1,128]{1,2,0:T(8,128)(2,1)S(1)}, bf16[6,1,128]{1,2,0:T(8,128)(2,1)S(1)}, u32[]{:S(2)}, u32[]{:S(2)}) %collective-permute-start.3) | collective-permute-done | bytes 1568 | tf_op jit(solution)/shard_map/ppermute | solution.py:15
  130.0 5.8 copy.36
  135.8 9.4 %fusion.13 = f32[1,4,256,4,32]{4,0,3,2,1:T(1,128)S(1)} fusion(bf16[1,6,258,4,32]{4,0,3,2,1:T(2,128)(2,1)} %copy.36, bf16[3,3,32,4,32]{4,3,2,1,0:T(4,128)(2,1)} %shard_map.94), kind=kOutput, calls=%fused_computation.39 | convolution fusion | flops 75497472 | bytes 994304 | tf_op jit(solution)/shard_map/conv_general_dilated | solution.py:26
  145.3 3.5 copy.38
  152.2 3.3 collective-permute-start.4
  157.5 4.3 collective-permute-done.5
  161.8 3.5 collective-permute-start.6
  172.1 5.9 copy.44
  178.0 13.8 %convolution_reduce_fusion = f32[4,256,4,32]{3,2,1,0:T(4,128)S(1)} fusion(bf16[1,6,258,4,32]{4,0,3,2,1:T(2,128)(2,1)} %copy.44, bf16[3,3,32,4,32]{4,3,2,1,0:T(4,128)(2,1)} %rev.6), kind=kOutput, calls=%fused_computation.2 | convolution fusion | flops 75497472 | bytes 994304 | tf_op jit(solution)/shard_map/conv_general_dilated | solution.py:26
  194.9 4.0 convolution_bitcast_fusion
  199.0 3.4 convolution_bitcast_fusion.1
  202.4 40.0 %reduce-scatter.9.cloned.1.call-done = f32[256,128]{0,1:T(8,128)} async-done(((f32[2048,128]{0,1:T(8,128)}), f32[256,128]{0,1:T(8,128)}) %reduce-scatter.9.cloned.1.call-update) | async-done | bytes 131088 | tf_op jit(solution)/shard_map/reduce_scatter | solution.py:130
  242.4 44.5 %reduce-scatter.11.cloned.1.call-done = f32[128,256]{1,0:T(8,128)} async-done(((f32[1024,256]{1,0:T(8,128)}), f32[128,256]{1,0:T(8,128)}) %reduce-scatter.11.cloned.1.call-update) | async-done | bytes 131088 | tf_op jit(solution)/shard_map/reduce_scatter | solution.py:131
  286.9 3.2 convolution_convert_fusion
  315.6 21.3 %all-reduce.6.cloned.1.call-done = (f32[256,128]{0,1:T(8,128)}, f32[128,256]{1,0:T(8,128)}) async-done(((f32[256,128]{0,1:T(8,128)}, f32[128,256]{1,0:T(8,128)}), (f32[256,128]{0,1:T(8,128)}, f32[128,256]{1,0:T(8,128)})) %all-reduce.6.cloned.1.call-update) | async-done | bytes 262160 | tf_op jit(solution)/shard_map/psum | solution.py:128
  338.7 59.3 %reduce-scatter.7.cloned.1.call-done = bf16[4,256,256]{2,1,0:T(8,128)(2,1)} async-done(((bf16[4,256,2048]{2,1,0:T(8,128)(2,1)}), bf16[4,256,256]{2,1,0:T(8,128)(2,1)}) %reduce-scatter.7.cloned.1.call-update) | async-done | bytes 524304 | tf_op jit(solution)/shard_map/reduce_scatter | solution.py:120
  400.1 290.7 %all-reduce.4.cloned.1.call-done = f32[3,3,32,128]{3,2,1,0:T(8,128)} async-done(((f32[3,3,32,128]{3,2,1,0:T(8,128)}), f32[3,3,32,128]{3,2,1,0:T(8,128)}) %all-reduce.4.cloned.1.call-update) | async-done | bytes 147472 | tf_op jit(solution)/shard_map/psum | solution.py:127
  (114 shorter events, 58.5 us)
Async XLA Ops:
  7.2 81.9 %all-gather.3.cloned.1.call-start = ((), (), s32[]{:S(2)}) async-start(), calls=%async_computation.4 | async-start | bytes 4718592 | tf_op jit(solution)/shard_map/all_gather | solution.py:76
  7.9 142.2 %reduce-scatter.5.cloned.1.call-start = ((), (), s32[]{:S(2)}) async-start(), calls=%async_computation.6 | async-start | bytes 4718592 | tf_op jit(solution)/shard_map/reduce_scatter | solution.py:96
  51.4 147.6 %all-gather.5.cloned.1.call-start = ((), (), s32[]{:S(2)}) async-start(), calls=%async_computation.5 | async-start | bytes 2359296 | tf_op jit(solution)/shard_map/all_gather | solution.py:87
  89.1 4.4 copy-start
  93.5 16.3 %copy-start.12 = (bf16[3,3,32,128]{3,2,1,0:T(8,128)(2,1)S(1)}, bf16[3,3,32,128]{3,2,1,0:T(8,128)(2,1)}, u32[]{:S(2)}) copy-start(bf16[3,3,32,128]{3,2,1,0:T(8,128)(2,1)} %param.7) | copy-start | bytes 221188
  93.5 4.8 collective-permute-start
  96.4 6.2 collective-permute-start.1
  98.3 4.6 copy-start.7
  103.2 15.5 %collective-permute-start.2 = (bf16[6,1,128]{1,2,0:T(8,128)(2,1)S(1)}, bf16[6,1,128]{1,2,0:T(8,128)(2,1)S(1)}, u32[]{:S(2)}, u32[]{:S(2)}) collective-permute-start(bf16[6,1,128]{1,2,0:T(8,128)(2,1)S(1)} %get-tuple-element.29), channel_id=1, source_target_pairs={{0,8},{8,16},{16,24},{24,32},{32,40},{40,48},{48,56},{1,9},{9,17},... | collective-permute-start | bytes 4616 | tf_op jit(solution)/shard_map/ppermute | solution.py:12
  106.6 22.7 %collective-permute-start.3 = (bf16[6,1,128]{1,2,0:T(8,128)(2,1)S(1)}, bf16[6,1,128]{1,2,0:T(8,128)(2,1)S(1)}, u32[]{:S(2)}, u32[]{:S(2)}) collective-permute-start(bf16[6,1,128]{1,2,0:T(8,128)(2,1)S(1)} %get-tuple-element.30), channel_id=1, source_target_pairs={{8,0},{16,8},{24,16},{32,24},{40,32},{48,40},{56,48},{9,1},{17,9},... | collective-permute-start | bytes 4616 | tf_op jit(solution)/shard_map/ppermute | solution.py:15
  118.7 17.1 %copy-start.4 = (bf16[6,1,128]{1,2,0:T(8,128)(2,1)}, bf16[6,1,128]{1,2,0:T(8,128)(2,1)S(1)}, u32[]{:S(2)}) copy-start(bf16[6,1,128]{1,2,0:T(8,128)(2,1)S(1)} %collective-permute-done.2) | copy-start | bytes 4612
  148.8 19.0 %copy-start.3 = (bf16[3,3,32,4,32]{4,3,2,1,0:T(4,128)(2,1)S(1)}, bf16[3,3,32,4,32]{4,3,2,1,0:T(4,128)(2,1)}, u32[]{:S(2)}) copy-start(bf16[3,3,32,4,32]{4,3,2,1,0:T(4,128)(2,1)} %shard_map.94) | copy-start | bytes 221188
  152.2 90.2 %reduce-scatter.9.cloned.1.call-start = ((), (), s32[]{:S(2)}) async-start(), calls=%async_computation.9 | async-start | bytes 1179648 | tf_op jit(solution)/shard_map/reduce_scatter | solution.py:130
  152.2 5.2 collective-permute-start.4
  155.6 6.2 collective-permute-start.5
  161.8 7.4 %collective-permute-start.6 = (bf16[6,1,128]{2,1,0:T(2,128)(2,1)S(1)}, bf16[6,1,128]{2,1,0:T(2,128)(2,1)S(1)}, u32[]{:S(2)}, u32[]{:S(2)}) collective-permute-start(bf16[6,1,128]{2,1,0:T(2,128)(2,1)S(1)} %get-tuple-element.27), channel_id=1, source_target_pairs={{0,8},{8,16},{16,24},{24,32},{32,40},{40,48},{48,56},{1,9},{9,17},... | collective-permute-start | bytes 4616 | tf_op jit(solution)/shard_map/ppermute | solution.py:12
  165.3 6.4 collective-permute-start.7
  194.9 4.1 copy-start.2
  198.9 88.0 %copy-start.1 = (bf16[2048,128]{1,0:T(8,128)(2,1)S(1)}, bf16[2048,128]{1,0:T(8,128)(2,1)}, u32[]{:S(2)}) copy-start(bf16[2048,128]{1,0:T(8,128)(2,1)} %copy-done) | copy-start | bytes 1572868
  198.9 88.0 %reduce-scatter.11.cloned.1.call-start = ((), (), s32[]{:S(2)}) async-start(), calls=%async_computation.10 | async-start | bytes 1179648 | tf_op jit(solution)/shard_map/reduce_scatter | solution.py:131
  202.4 134.6 %all-reduce.6.cloned.1.call-start = ((), (), s32[]{:S(2)}) async-start(), calls=%async_computation.11 | async-start | bytes 524288 | tf_op jit(solution)/shard_map/psum | solution.py:128
  286.9 111.1 %reduce-scatter.7.cloned.1.call-start = ((), (), s32[]{:S(2)}) async-start(), calls=%async_computation.7 | async-start | bytes 4718592 | tf_op jit(solution)/shard_map/reduce_scatter | solution.py:120
  290.2 400.7 %all-reduce.4.cloned.1.call-start = ((), (), s32[]{:S(2)}) async-start(), calls=%async_computation.8 | async-start | bytes 294912 | tf_op jit(solution)/shard_map/psum | solution.py:127
  337.0 355.5 %copy-start.11 = (f32[128,256]{1,0:T(8,128)S(1)}, f32[128,256]{1,0:T(8,128)}, u32[]{:S(2)}) copy-start(f32[128,256]{1,0:T(8,128)} %get-tuple-element.46) | copy-start | bytes 393220
  (6 other events, 5.5 us)
Sparse Core Ops, SparseCore 0:
  9.8 60.3 all-gather.2
  72.7 76.7 reduce-scatter.4
  152.3 42.8 all-gather.4
  199.0 43.3 reduce-scatter.8
  244.8 42.0 reduce-scatter.10
  289.1 47.8 all-reduce.5
  339.7 58.2 reduce-scatter.6
  401.4 289.4 all-reduce.3
where the time goes:
time: 701 us; the launch traced here: 700 us
  waiting for transfers between devices  487 us (69%)
  blocking collectives  76.5 us (11%)
  matrix products  49 us (7%)
  local copies, waits for them, and re-layouts  43.4 us (6%)
  starting transfers between devices  22 us (3%)
  between operations  14.5 us (2%)
  other arithmetic  7.29 us (1%)
    psum x1, waiting for transfers between devices, body(): group_grad = lax.psum(kernel_part, ('rows', 'chan'))  291 us
    reduce_scatter x1, waiting for transfers between devices, body(): lax.psum_scatter(input_terms.reshape(rows_here, cols_here, input_terms.sh...  59.3 us
    reduce_scatter x1, waiting for transfers between devices, body(): lax.psum_scatter(third_total, 'chan', scatter_dimension=0, tiled=True)  44.5 us
    reduce_scatter x1, waiting for transfers between devices, body(): lax.psum_scatter(first_total, 'chan', scatter_dimension=0, tiled=True)  40 us
    all_gather x1, blocking collectives, body(): lax.all_gather(third_weight, 'chan', axis=0, tiled=True)  39.6 us
    all_gather x1, blocking collectives, body(): lax.all_gather(first_weight, 'chan', axis=0, tiled=True)  36.9 us
    conv_general_dilated x2, matrix products, group_conv(): lax.conv_general_dilated(padded[None], kernel, (1, 1), 'VALID', dimension...  23.3 us
    ppermute x4, waiting for transfers between devices, extended(): lax.ppermute(lax.slice_in_dim(block, 0, width, axis=dim), axis, backward)  21.5 us
  transfers between devices with their start and end apart: 16, of which 12 were waited for; matrix products, arithmetic and copies ran while one was open for 13% of the time, Pallas kernels for 0%

commit v1 on v0

v1 whole, which is shorter than its diff:
```python
import jax
import jax.numpy as jnp
from jax import lax
from jax.experimental import pallas as pl
from jax.experimental.pallas import tpu as pltpu
from jax.sharding import PartitionSpec as P

F32 = jnp.float32
BF16 = jnp.bfloat16
VMEM = pl.BlockSpec(memory_space=pltpu.VMEM)
SMEM = pl.BlockSpec(memory_space=pltpu.SMEM)


def dot(a, b, ca=1, cb=0):
    return lax.dot_general(a, b, (((ca,), (cb,)), ((), ())), preferred_element_type=F32)


def call(kernel, outs, n_smem, args, scratch=()):
    return pl.pallas_call(
        kernel,
        out_shape=[jax.ShapeDtypeStruct(s, d) for s, d in outs],
        in_specs=[SMEM] * n_smem + [VMEM] * (len(args) - n_smem),
        out_specs=[VMEM] * len(outs),
        scratch_shapes=list(scratch),
        compiler_params=pltpu.CompilerParams(vmem_limit_bytes=48 * 2**20),
    )(*args)


def block_of(ref, zone, step, size):
    which = lax.rem(zone + step, 4)
    return ref[pl.ds(pl.multiple_of(which * size, size), size), :]


def logistic(v):
    return 1.0 / (1.0 + jnp.exp(-v))


def slope(v):
    s = logistic(v)
    return s * (1.0 + v * (1.0 - s))


def first_kernel(zone_ref, own, left, right, far_a, far_b, w1, pre, act):
    zone = zone_ref[0]
    half = far_a.shape[0]
    size = own.shape[1]
    for part, far in ((0, far_a), (1, far_b)):
        rows = pl.ds(part * half, half)
        v = dot(own[rows, :], block_of(w1, zone, 0, size))
        v += dot(left[rows, :], block_of(w1, zone, 3, size))
        v += dot(right[rows, :], block_of(w1, zone, 1, size))
        v += dot(far[...], block_of(w1, zone, 2, size))
        pre[rows, :] = v
        act[rows, :] = (v * logistic(v)).astype(BF16)


def mid_kernel(zone_ref, grad, w3, p0, p1, p3, p2):
    zone = zone_ref[0]
    size = p0.shape[1]
    g = grad[...]
    p2[...] = dot(g, block_of(w3, zone, 2, size), 1, 1).astype(BF16)
    p1[...] = dot(g, block_of(w3, zone, 1, size), 1, 1).astype(BF16)
    p3[...] = dot(g, block_of(w3, zone, 3, size), 1, 1).astype(BF16)
    p0[...] = dot(g, block_of(w3, zone, 0, size), 1, 1)


def shifted(rows_total, cols, up, mid, down, low, high, out):
    chans = mid.shape[1]
    x = jnp.concatenate([up[...].astype(F32), mid[...].astype(F32), down[...].astype(F32)], axis=0)
    n = rows_total * cols
    col = lax.rem(lax.broadcasted_iota(jnp.int32, (n, chans), 0), cols)

    def spread(edge):
        parts = [jnp.broadcast_to(edge[i : i + 1, :], (cols, chans)) for i in range(rows_total)]
        return jnp.concatenate(parts, axis=0)

    out[1] = x.astype(BF16)
    out[0] = jnp.where(col == 0, spread(low), pltpu.roll(x, 1, 0)).astype(BF16)
    out[2] = jnp.where(col == cols - 1, spread(high), pltpu.roll(x, n - 1, 0)).astype(BF16)


def group_kernel(up, mid, down, low, high, wd, pre, act, xs):
    n = mid.shape[0]
    cols = up.shape[0]
    shifted(n // cols + 2, cols, up, mid, down, low, high, xs)
    total = jnp.zeros(pre.shape, F32)
    for a in range(3):
        for b in range(3):
            total += dot(xs[b, a * cols : a * cols + n, :], wd[3 * a + b])
    pre[...] = total
    act[...] = (total * logistic(total)).astype(BF16)


def group_grad_kernel(xs, delta, out):
    n, chans = delta.shape
    cols = xs.shape[1] - n
    cols = cols // 2
    size = out.shape[1]
    d = delta[...]
    row_group = lax.broadcasted_iota(jnp.int32, (chans, chans), 0) // size
    col_group = lax.broadcasted_iota(jnp.int32, (chans, chans), 1) // size
    keep = row_group == col_group
    for a in range(3):
        for b in range(3):
            full = dot(xs[b, a * cols : a * cols + n, :], d, 0, 0)
            full = jnp.where(keep, full, 0.0)
            total = full[0:size]
            for g in range(1, chans // size):
                total += full[g * size : (g + 1) * size]
            out[3 * a + b] = total


def back_kernel(zone_ref, up, mid, down, low, high, wd, pre, w1, fdelta, p0, p1, p3, p2, ds):
    zone = zone_ref[0]
    n = mid.shape[0]
    cols = up.shape[0]
    shifted(n // cols + 2, cols, up, mid, down, low, high, ds)
    total = jnp.zeros(pre.shape, F32)
    for a in range(3):
        for b in range(3):
            at = (2 - a) * cols
            total += dot(ds[2 - b, at : at + n, :], wd[3 * a + b], 1, 1)
    d = (total * slope(pre[...])).astype(BF16)
    fdelta[...] = d
    size = p0.shape[1]
    p2[...] = dot(d, block_of(w1, zone, 2, size), 1, 1).astype(BF16)
    p1[...] = dot(d, block_of(w1, zone, 1, size), 1, 1).astype(BF16)
    p3[...] = dot(d, block_of(w1, zone, 3, size), 1, 1).astype(BF16)
    p0[...] = dot(d, block_of(w1, zone, 0, size), 1, 1).astype(BF16)


def first_grad_kernel(zone_ref, own, left, right, far_a, far_b, delta, out):
    zone = zone_ref[0]
    half = far_a.shape[0]
    size = own.shape[1]
    d = delta[...]

    def put(step, v):
        which = lax.rem(zone + step, 4)
        out[pl.ds(pl.multiple_of(which * size, size), size), :] = v.astype(BF16)

    put(0, dot(own[...], d, 0, 0))
    put(3, dot(left[...], d, 0, 0))
    put(1, dot(right[...], d, 0, 0))
    put(2, dot(far_a[...], d[:half], 0, 0) + dot(far_b[...], d[half:], 0, 0))


def third_kernel(zone_ref, own, left, right, far_a, far_b, w3, grad, images, block_out, part):
    zone = zone_ref[0]
    half = far_a.shape[0]
    size = own.shape[1]
    for p, far in ((0, far_a), (1, far_b)):
        rows = pl.ds(p * half, half)
        v = dot(own[rows, :], block_of(w3, zone, 0, size))
        v += dot(left[rows, :], block_of(w3, zone, 3, size))
        v += dot(right[rows, :], block_of(w3, zone, 1, size))
        v += dot(far[...], block_of(w3, zone, 2, size))
        block_out[rows, :] = (images[rows, :].astype(F32) + v).astype(BF16)
    g = grad[...]

    def put(step, v):
        which = lax.rem(zone + step, 4)
        part[pl.ds(pl.multiple_of(which * size, size), size), :] = v.astype(BF16)

    put(0, dot(own[...], g, 0, 0))
    put(3, dot(left[...], g, 0, 0))
    put(1, dot(right[...], g, 0, 0))
    put(2, dot(far_a[...], g[:half], 0, 0) + dot(far_b[...], g[half:], 0, 0))


def body(images, first_weight, group_weight, third_weight, out_grad):
    rows_here, cols_all, chans_own = images.shape
    filt = lax.axis_size("filt")
    chan = lax.axis_size("chan")
    rows = lax.axis_size("rows")
    zones = filt // 2
    me = lax.axis_index("filt")
    core = lax.rem(me, 2)
    zone = (me // 2).astype(jnp.int32).reshape(1)
    cols = cols_all // 2
    pixels = rows_here * cols

    swap = [(i, i ^ 1) for i in range(filt)]
    zplus = [(z * 2 + c, (z + 1) % zones * 2 + c) for z in range(zones) for c in range(2)]
    zminus = [(t, s) for s, t in zplus]

    def halves(v, axis):
        n = v.shape[axis] // 2
        keep = lax.dynamic_slice_in_dim(v, core * n, n, axis)
        send = lax.dynamic_slice_in_dim(v, (1 - core) * n, n, axis)
        return keep, send

    def joined(keep, got, axis):
        return jnp.where(
            core == 0,
            jnp.concatenate([keep, got], axis),
            jnp.concatenate([got, keep], axis),
        )

    def core_swap(v):
        return lax.ppermute(v, "filt", swap)

    def split_pixels(v):
        keep, send = halves(v, 1)
        return joined(keep, core_swap(send), 2).reshape(pixels, 2 * chans_own)

    def merge_pixels(v):
        v = v.reshape(rows_here, cols, 2 * chans_own)
        keep, send = halves(v, 2)
        return joined(keep, core_swap(send), 1)

    def ring_gather(v):
        half = v.shape[0] // 2
        left = lax.ppermute(v, "filt", zplus)
        right = lax.ppermute(v, "filt", zminus)
        far_a = lax.ppermute(left[:half], "filt", zplus)
        far_b = lax.ppermute(right[half:], "filt", zminus)
        return v, left, right, far_a, far_b

    def ring_scatter(p1, p3, p2):
        half = p2.shape[0] // 2
        plus_b = lax.ppermute(p1[half:], "filt", zplus)
        got_a = lax.ppermute(p2[:half], "filt", zplus)
        minus_a = lax.ppermute(p3[:half], "filt", zminus)
        got_b = lax.ppermute(p2[half:], "filt", zminus)
        plus_a = lax.ppermute(
            (p1[:half].astype(F32) + got_a.astype(F32)).astype(BF16), "filt", zplus
        )
        minus_b = lax.ppermute(
            (p3[half:].astype(F32) + got_b.astype(F32)).astype(BF16), "filt", zminus
        )
        low = plus_a.astype(F32) + minus_a.astype(F32)
        high = plus_b.astype(F32) + minus_b.astype(F32)
        return jnp.concatenate([low, high], axis=0)

    col_next = [
        ((k * filt) + z * 2 + c, (k * filt + z * 2 + 1) if c == 0 else ((k + 1) * filt + z * 2))
        for k in range(chan)
        for z in range(zones)
        for c in range(2)
        if c == 0 or k < chan - 1
    ]
    col_prev = [(t, s) for s, t in col_next]
    row_next = [(i, i + 1) for i in range(rows - 1)]
    row_prev = [(t, s) for s, t in row_next]

    def halo(v):
        up = lax.ppermute(v[pixels - cols :], "rows", row_next)
        down = lax.ppermute(v[:cols], "rows", row_prev)
        own = v.reshape(rows_here, cols, v.shape[1])
        first = jnp.concatenate([up[:1], own[:, 0], down[:1]], axis=0)
        last = jnp.concatenate([up[cols - 1 :], own[:, cols - 1], down[cols - 1 :]], axis=0)
        low = lax.ppermute(last, ("chan", "filt"), col_next)
        high = lax.ppermute(first, ("chan", "filt"), col_prev)
        return up, v, down, low.astype(F32), high.astype(F32)

    def chan_gather(v):
        return lax.all_to_all(jnp.broadcast_to(v[None], (chan,) + v.shape), "chan", 0, 0)

    img = split_pixels(images)
    blocks = ring_gather(img)
    grad = split_pixels(out_grad)

    rows1, mid_own = first_weight.shape
    rows3, c_own = third_weight.shape
    wide = chan_gather(
        jnp.concatenate(
            [first_weight]
            + [third_weight[:, i : i + mid_own] for i in range(0, c_own, mid_own)],
            axis=0,
        )
    )
    wide_other = core_swap(wide)
    w1 = joined(wide[:, :rows1], wide_other[:, :rows1], 2).reshape(chan * rows1, 2 * mid_own)

    def third_of(w):
        return jnp.concatenate(
            [
                w[:, rows1 + i * rows3 : rows1 + (i + 1) * rows3]
                for i in range(c_own // mid_own)
            ],
            axis=2,
        )

    w3 = joined(third_of(wide), third_of(wide_other), 2).reshape(chan * rows3, 2 * c_own)

    size = group_weight.shape[2]
    taps = group_weight.reshape(9, size, mid_own)
    taps = joined(taps, core_swap(taps), 2)
    mid_here = 2 * mid_own
    diag = (jnp.arange(mid_here) // size)[:, None] == (jnp.arange(mid_here) // size)[None, :]
    wd = jnp.where(diag[None], jnp.tile(taps, (1, mid_here // size, 1)), 0).astype(BF16)

    m0, m1, m3, m2 = call(
        mid_kernel,
        [((pixels, mid_here), F32)] + [((pixels, mid_here), BF16)] * 3,
        1,
        (zone, grad, w3),
    )
    pre_first, act_first = call(
        first_kernel,
        [((pixels, mid_here), F32), ((pixels, mid_here), BF16)],
        1,
        (zone, *blocks, w1),
    )
    mid_rest = ring_scatter(m1, m3, m2)
    pre_group, act_group, xs = call(
        group_kernel,
        [
            ((pixels, mid_here), F32),
            ((pixels, mid_here), BF16),
            ((3, pixels + 2 * cols, mid_here), BF16),
        ],
        0,
        (*halo(act_first), wd),
    )
    delta = ((m0 + mid_rest) * slope(pre_group)).astype(BF16)
    delta_halo = halo(delta)
    acts = ring_gather(act_group)
    (group_part,) = call(group_grad_kernel, [((9, size, mid_here), F32)], 0, (xs, delta))

    first_delta, b0, b1, b3, b2 = call(
        back_kernel,
        [((pixels, mid_here), BF16)] + [((pixels, 2 * chans_own), BF16)] * 4,
        1,
        (zone, *delta_halo, wd, pre_first, w1),
        [pltpu.VMEM((3, pixels + 2 * cols, mid_here), BF16)],
    )
    back_rest = ring_scatter(b1, b3, b2)
    block_wide, third_part = call(
        third_kernel,
        [((pixels, 2 * chans_own), BF16), ((chan * rows3, 2 * c_own), BF16)],
        1,
        (zone, *acts, w3, grad, img),
    )
    block_out = merge_pixels(block_wide)
    (first_part,) = call(
        first_grad_kernel, [((chan * rows1, mid_here), BF16)], 1, (zone, *blocks, first_delta)
    )

    def over_cores(v, axis):
        keep, send = halves(v, axis)
        return (keep.astype(F32) + core_swap(send).astype(F32)).astype(BF16)

    third_half = over_cores(third_part, 1).reshape(chan, rows3, c_own)
    first_half = over_cores(first_part, 1).reshape(chan, rows1, mid_own)
    group_half = over_cores(group_part.astype(BF16), 2).reshape(9 * size, mid_own)
    packed = jnp.concatenate(
        [first_half]
        + [third_half[:, :, i : i + mid_own] for i in range(0, c_own, mid_own)]
        + [jnp.broadcast_to(group_half[None], (chan,) + group_half.shape)],
        axis=1,
    )
    packed = lax.all_to_all(packed, "chan", 0, 0)
    packed = jnp.sum(packed.astype(F32), axis=0).astype(BF16)
    ring = [(i, (i + 1) % rows) for i in range(rows)]
    back_ring = [(t, s) for s, t in ring]
    across = [(i, (i + 2) % rows) for i in range(rows)]
    before = lax.ppermute(packed, "rows", ring).astype(F32)
    after = lax.ppermute(packed, "rows", back_ring).astype(F32)
    opposite = lax.ppermute(packed, "rows", across).astype(F32)
    summed = (packed.astype(F32) + opposite) + (before + after)
    first_grad = summed[:rows1]
    third_grad = jnp.concatenate(
        [summed[rows1 + i * rows3 : rows1 + (i + 1) * rows3] for i in range(c_own // mid_own)],
        axis=1,
    )
    group_grad = summed[rows1 + rows3 * (c_own // mid_own) :].reshape(group_weight.shape)

    back = (b0.astype(F32) + back_rest).astype(BF16)
    images_grad = out_grad.astype(F32) + merge_pixels(back).astype(F32)
    return (block_out, images_grad, first_grad, group_grad, third_grad)


def solution(mesh):
    in_specs = (
        P("rows", "chan", "filt"),
        P("chan", "filt"),
        P(None, None, None, "filt"),
        P("chan", "filt"),
        P("rows", "chan", "filt"),
    )
    out_specs = (
        P("rows", "chan", "filt"),
        P("rows", "chan", "filt"),
        P("chan", "filt"),
        P(None, None, None, "filt"),
        P("chan", "filt"),
    )
    return jax.shard_map(body, mesh=mesh, in_specs=in_specs, out_specs=out_specs, check_vma=False)
```

time: 701 us -> 241 us (0.34)
  waiting for transfers between devices: 487 us -> 116 us
  blocking collectives: 76.5 us -> 0 us
  starting transfers between devices: 22 us -> 90.7 us
  matrix products: 49 us -> 0 us
  local copies, waits for them, and re-layouts: 43.4 us -> 12.2 us
  between operations: 14.5 us -> 1.48 us
  Pallas kernels: 0 us -> 8.51 us
    psum x2 -> x0, waiting for transfers between devices: 312 us -> none  [the longest x1 291 us: body(): group_grad = lax.psum(kernel_part, ('rows', 'chan'))]
    reduce_scatter x4 -> x0, waiting for transfers between devices: 144 us -> none  [the longest x1 59.3 us: body(): lax.psum_scatter(input_terms.reshape(rows_here, cols_here, input_terms.sh...]
    all_gather x2 -> x0, blocking collectives: 76.5 us -> none  [the longest x1 39.6 us: body(): lax.all_gather(third_weight, 'chan', axis=0, tiled=True)]
    ppermute x8 -> x40, waiting for transfers between devices: 30.6 us -> 101 us  [the longest x2 28.7 us: ring_scatter(): got_b = lax.ppermute(p2[half:], 'filt', zminus)]
    ppermute x8 -> x40, starting transfers between devices: 21.4 us -> 75.8 us  [the longest x2 10.1 us: ring_gather(): right = lax.ppermute(v, 'filt', zminus)]
    dot_general x15 -> x0, matrix products: 25.7 us -> none  [the longest x1 4.41 us: body(): jnp.dot(flat_images, first_panel, preferred_element_type=jnp.float32)]
    conv_general_dilated x2 -> x0, matrix products: 23.3 us -> none  [group_conv(): lax.conv_general_dilated(padded[None], kernel, (1, 1), 'VALID', dimension...]
    all_to_all x0 -> x2, starting transfers between devices: none -> 15 us  [the longest x1 8.91 us: body(): packed = lax.all_to_all(packed, 'chan', 0, 0)]
  transfers between devices with their start and end apart: 16 -> 42, of which waited for: 12 -> 19; matrix products, arithmetic and copies ran while one was open for 13% -> 5% of each run, Pallas kernels for 0% -> 4%
where the time goes in v1:
time: 241 us; the launch traced here: 239 us
  waiting for transfers between devices  116 us (48%)
  starting transfers between devices  90.7 us (38%)
  local copies, waits for them, and re-layouts  12.2 us (5%)
  other arithmetic  9.95 us (4%)
  Pallas kernels  8.51 us (4%)
    ppermute x2, waiting for transfers between devices, ring_scatter(): got_b = lax.ppermute(p2[half:], 'filt', zminus)  28.7 us
    ppermute x2, waiting for transfers between devices, ring_gather(): right = lax.ppermute(v, 'filt', zminus)  20.7 us
    ppermute x2, waiting for transfers between devices, ring_scatter(): lax.ppermute((p3[half:].astype(F32) + got_b.astype(F32)).astype(BF16), 'f...  14.5 us
    all_to_all x1, waiting for transfers between devices, chan_gather(): lax.all_to_all(jnp.broadcast_to(v[None], (chan,) + v.shape), 'chan', 0, 0)  14.4 us
    ppermute x2, waiting for transfers between devices, ring_gather(): far_b = lax.ppermute(right[half:], 'filt', zminus)  11.2 us
    ppermute x2, starting transfers between devices, ring_gather(): right = lax.ppermute(v, 'filt', zminus)  10.1 us
    ppermute x2, starting transfers between devices, ring_scatter(): lax.ppermute((p3[half:].astype(F32) + got_b.astype(F32)).astype(BF16), 'f...  9.34 us
    ppermute x2, starting transfers between devices, ring_gather(): far_b = lax.ppermute(right[half:], 'filt', zminus)  9.31 us
  transfers between devices with their start and end apart: 42, of which 19 were waited for; matrix products, arithmetic and copies ran while one was open for 5% of the time, Pallas kernels for 4%

profile of v1, /device:TPU:32, one launch (start us, length us, event | category | flops | bytes accessed | tf_op | source)
XLA Modules:
  0.0 238.8 jit_solution(16498733355637340589)
XLA Ops:
  3.4 6.1 %all-to-all-start = ((bf16[8,512,128]{2,1,0:T(8,128)(2,1)}), bf16[8,512,128]{2,1,0:T(8,128)(2,1)S(1)}, u32[]{:S(2)}, u32[]{:S(2)}) async-start(bf16[8,512,128]{2,1,0:T(8,128)(2,1)} %broadcast_in_dim.28), calls=%async_computation | async-start | bytes 2097152 | tf_op jit(solution)/shard_map/all_to_all | solution.py:258
  9.6 14.4 %all-to-all-done = bf16[8,512,128]{2,1,0:T(8,128)(2,1)S(1)} async-done(((bf16[8,512,128]{2,1,0:T(8,128)(2,1)}), bf16[8,512,128]{2,1,0:T(8,128)(2,1)S(1)}, u32[]{:S(2)}, u32[]{:S(2)}) %all-to-all-start) | async-done | bytes 1048608 | tf_op jit(solution)/shard_map/all_to_all | solution.py:258
  24.6 5.5 %collective-permute-start.2 = (bf16[512,512]{1,0:T(8,128)(2,1)S(1)}, bf16[512,512]{1,0:T(8,128)(2,1)S(1)}, u32[]{:S(2)}, u32[]{:S(2)}) collective-permute-start(bf16[512,512]{1,0:T(8,128)(2,1)S(1)} %maximum_select_fusion.2.own.images), channel_id=1, source_target_pairs={{2,0},{3,1},{4,2},{5,3},{6,4},{7,5},{0,6},{1,7},{10,8},{11,9},{12,... | collective-permute-start | bytes 1572872 | tf_op jit(solution)/shard_map/ppermute | solution.py:215
  33.9 18.5 %collective-permute-done.2.right = bf16[512,512]{1,0:T(8,128)(2,1)S(1)} collective-permute-done((bf16[512,512]{1,0:T(8,128)(2,1)S(1)}, bf16[512,512]{1,0:T(8,128)(2,1)S(1)}, u32[]{:S(2)}, u32[]{:S(2)}) %collective-permute-start.2) | collective-permute-done | bytes 524320 | tf_op jit(solution)/shard_map/ppermute | solution.py:215
  52.4 4.7 %collective-permute-start.4 = (bf16[256,512]{1,0:T(8,128)(2,1)S(1)}, bf16[256,512]{1,0:T(8,128)(2,1)S(1)}, u32[]{:S(2)}, u32[]{:S(2)}) collective-permute-start(bf16[256,512]{1,0:T(8,128)(2,1)S(1)} %slice.185), channel_id=1, source_target_pairs={{2,0},{3,1},{4,2},{5,3},{6,4},{7,5},{0,6},{1,7},{10,8},{11,9},{12,... | collective-permute-start | bytes 786440 | tf_op jit(solution)/shard_map/ppermute | solution.py:217
  58.8 8.8 %collective-permute-done.4.far_b = bf16[256,512]{1,0:T(8,128)(2,1)S(1)} collective-permute-done((bf16[256,512]{1,0:T(8,128)(2,1)S(1)}, bf16[256,512]{1,0:T(8,128)(2,1)S(1)}, u32[]{:S(2)}, u32[]{:S(2)}) %collective-permute-start.4) | collective-permute-done | bytes 262176 | tf_op jit(solution)/shard_map/ppermute | solution.py:217
  67.6 4.0 %collective-permute-done.3.far_a = bf16[256,512]{1,0:T(8,128)(2,1)S(1)} collective-permute-done((bf16[256,512]{1,0:T(8,128)(2,1)S(1)}, bf16[256,512]{1,0:T(8,128)(2,1)S(1)}, u32[]{:S(2)}, u32[]{:S(2)}) %collective-permute-start.3) | collective-permute-done | bytes 262176 | tf_op jit(solution)/shard_map/ppermute | solution.py:216
  73.7 4.5 %collective-permute-start.6 = (bf16[128,256]{1,0:T(8,128)(2,1)S(1)}, bf16[128,256]{1,0:T(8,128)(2,1)S(1)}, u32[]{:S(2)}, u32[]{:S(2)}) collective-permute-start(bf16[128,256]{1,0:T(8,128)(2,1)S(1)} %get-tuple-element.64), channel_id=1, source_target_pairs={{0,64},{64,128},{128,192},{1,65},{65,129},{129,193},{2,66},{66,130... | collective-permute-start | bytes 196616 | tf_op jit(solution)/shard_map/ppermute | solution.py:248
  82.7 3.6 %collective-permute-start.9 = (bf16[6,256]{1,0:T(8,128)(2,1)S(1)}, bf16[6,256]{1,0:T(8,128)(2,1)S(1)}, u32[]{:S(2)}, u32[]{:S(2)}) collective-permute-start(bf16[6,256]{1,0:T(8,128)(2,1)S(1)} %pad_maximum_fusion.4), channel_id=1, source_target_pairs={{1,0},{8,1},{3,2},{10,3},{5,4},{12,5},{7,6},{14,7},{9,8},{16,9},{1... | collective-permute-start | bytes 9224 | tf_op jit(solution)/shard_map/ppermute | solution.py:254
  86.6 4.2 %collective-permute-start.19 = (bf16[256,256]{1,0:T(8,128)(2,1)S(1)}, bf16[256,256]{1,0:T(8,128)(2,1)S(1)}, u32[]{:S(2)}, u32[]{:S(2)}) collective-permute-start(bf16[256,256]{1,0:T(8,128)(2,1)S(1)} %slice.160), channel_id=1, source_target_pairs={{2,0},{3,1},{4,2},{5,3},{6,4},{7,5},{0,6},{1,7},{10,8},{11,9},{12,... | collective-permute-start | bytes 393224 | tf_op jit(solution)/shard_map/ppermute | solution.py:224
  90.8 4.1 %collective-permute-start.21 = (bf16[256,256]{1,0:T(8,128)(2,1)S(1)}, bf16[256,256]{1,0:T(8,128)(2,1)S(1)}, u32[]{:S(2)}, u32[]{:S(2)}) collective-permute-start(bf16[256,256]{1,0:T(8,128)(2,1)S(1)} %get-tuple-element.60), channel_id=1, source_target_pairs={{2,0},{3,1},{4,2},{5,3},{6,4},{7,5},{0,6},{1,7},{10,8},{11,9},{12,... | collective-permute-start | bytes 393224 | tf_op jit(solution)/shard_map/ppermute | solution.py:225
  95.9 4.0 %collective-permute-done.21 = bf16[256,256]{1,0:T(8,128)(2,1)S(1)} collective-permute-done((bf16[256,256]{1,0:T(8,128)(2,1)S(1)}, bf16[256,256]{1,0:T(8,128)(2,1)S(1)}, u32[]{:S(2)}, u32[]{:S(2)}) %collective-permute-start.21) | collective-permute-done | bytes 131104 | tf_op jit(solution)/shard_map/ppermute | solution.py:225
  100.0 4.7 %collective-permute-start.22 = (bf16[256,256]{1,0:T(8,128)(2,1)S(1)}, bf16[256,256]{1,0:T(8,128)(2,1)S(1)}, u32[]{:S(2)}, u32[]{:S(2)}) collective-permute-start(bf16[256,256]{1,0:T(8,128)(2,1)S(1)} %add_convert_fusion.4), channel_id=1, source_target_pairs={{2,0},{3,1},{4,2},{5,3},{6,4},{7,5},{0,6},{1,7},{10,8},{11,9},{12,... | collective-permute-start | bytes 393224 | tf_op jit(solution)/shard_map/ppermute | solution.py:229
  104.7 4.4 %collective-permute-done.22 = bf16[256,256]{1,0:T(8,128)(2,1)S(1)} collective-permute-done((bf16[256,256]{1,0:T(8,128)(2,1)S(1)}, bf16[256,256]{1,0:T(8,128)(2,1)S(1)}, u32[]{:S(2)}, u32[]{:S(2)}) %collective-permute-start.22) | collective-permute-done | bytes 131104 | tf_op jit(solution)/shard_map/ppermute | solution.py:229
  110.9 4.5 %collective-permute-start.23 = (bf16[128,256]{1,0:T(8,128)(2,1)S(1)}, bf16[128,256]{1,0:T(8,128)(2,1)S(1)}, u32[]{:S(2)}, u32[]{:S(2)}) collective-permute-start(bf16[128,256]{1,0:T(8,128)(2,1)S(1)} %get-tuple-element.58), channel_id=1, source_target_pairs={{0,64},{64,128},{128,192},{1,65},{65,129},{129,193},{2,66},{66,130... | collective-permute-start | bytes 196616 | tf_op jit(solution)/shard_map/ppermute | solution.py:248
  122.9 4.7 %collective-permute-start.12 = (bf16[512,256]{1,0:T(8,128)(2,1)S(1)}, bf16[512,256]{1,0:T(8,128)(2,1)S(1)}, u32[]{:S(2)}, u32[]{:S(2)}) collective-permute-start(bf16[512,256]{1,0:T(8,128)(2,1)S(1)} %get-tuple-element.22.own), channel_id=1, source_target_pairs={{2,0},{3,1},{4,2},{5,3},{6,4},{7,5},{0,6},{1,7},{10,8},{11,9},{12,... | collective-permute-start | bytes 786440 | tf_op jit(solution)/shard_map/ppermute | solution.py:215
  137.5 4.6 %collective-permute-start.14 = (bf16[256,256]{1,0:T(8,128)(2,1)}, bf16[256,256]{1,0:T(8,128)(2,1)S(1)}, u32[]{:S(2)}, u32[]{:S(2)}) collective-permute-start(bf16[256,256]{1,0:T(8,128)(2,1)} %slice.195), channel_id=1, source_target_pairs={{2,0},{3,1},{4,2},{5,3},{6,4},{7,5},{0,6},{1,7},{10,8},{11,9},{12,... | collective-permute-start | bytes 393224 | tf_op jit(solution)/shard_map/ppermute | solution.py:217
  157.7 8.9 %all-to-all-start.1 = ((bf16[8,800,128]{2,1,0:T(8,128)(2,1)}), bf16[8,800,128]{2,1,0:T(8,128)(2,1)S(1)}, u32[]{:S(2)}, u32[]{:S(2)}) async-start(bf16[8,800,128]{2,1,0:T(8,128)(2,1)} %pad_maximum_fusion), calls=%async_computation.1 | async-start | bytes 3276800 | tf_op jit(solution)/shard_map/all_to_all | solution.py:354
  166.7 4.1 %collective-permute-start.31 = (bf16[256,512]{1,0:T(8,128)(2,1)S(1)}, bf16[256,512]{1,0:T(8,128)(2,1)S(1)}, u32[]{:S(2)}, u32[]{:S(2)}) collective-permute-start(bf16[256,512]{1,0:T(8,128)(2,1)S(1)} %get-tuple-element.46), channel_id=1, source_target_pairs={{2,0},{3,1},{4,2},{5,3},{6,4},{7,5},{0,6},{1,7},{10,8},{11,9},{12,... | collective-permute-start | bytes 786440 | tf_op jit(solution)/shard_map/ppermute | solution.py:225
  173.9 4.2 %collective-permute-done.27 = bf16[256,512]{1,0:T(8,128)(2,1)S(1)} collective-permute-done((bf16[256,512]{1,0:T(8,128)(2,1)S(1)}, bf16[256,512]{1,0:T(8,128)(2,1)S(1)}, u32[]{:S(2)}, u32[]{:S(2)}) %collective-permute-start.27) | collective-permute-done | bytes 262176 | tf_op jit(solution)/shard_map/ppermute | solution.py:223
  178.3 24.7 %collective-permute-done.31 = bf16[256,512]{1,0:T(8,128)(2,1)S(1)} collective-permute-done((bf16[256,512]{1,0:T(8,128)(2,1)S(1)}, bf16[256,512]{1,0:T(8,128)(2,1)S(1)}, u32[]{:S(2)}, u32[]{:S(2)}) %collective-permute-start.31) | collective-permute-done | bytes 262176 | tf_op jit(solution)/shard_map/ppermute | solution.py:225
  203.1 4.7 %collective-permute-start.32 = (bf16[256,512]{1,0:T(8,128)(2,1)S(1)}, bf16[256,512]{1,0:T(8,128)(2,1)S(1)}, u32[]{:S(2)}, u32[]{:S(2)}) collective-permute-start(bf16[256,512]{1,0:T(8,128)(2,1)S(1)} %add_convert_fusion.2), channel_id=1, source_target_pairs={{2,0},{3,1},{4,2},{5,3},{6,4},{7,5},{0,6},{1,7},{10,8},{11,9},{12,... | collective-permute-start | bytes 786440 | tf_op jit(solution)/shard_map/ppermute | solution.py:229
  208.7 10.1 %collective-permute-done.32 = bf16[256,512]{1,0:T(8,128)(2,1)S(1)} collective-permute-done((bf16[256,512]{1,0:T(8,128)(2,1)S(1)}, bf16[256,512]{1,0:T(8,128)(2,1)S(1)}, u32[]{:S(2)}, u32[]{:S(2)}) %collective-permute-start.32) | collective-permute-done | bytes 262176 | tf_op jit(solution)/shard_map/ppermute | solution.py:229
  227.0 6.2 %collective-permute-done.39 = bf16[800,128]{1,0:T(8,128)(2,1)S(1)} collective-permute-done((bf16[800,128]{1,0:T(8,128)(2,1)S(1)}, bf16[800,128]{1,0:T(8,128)(2,1)S(1)}, u32[]{:S(2)}, u32[]{:S(2)}) %collective-permute-start.39) | collective-permute-done | bytes 204832 | tf_op jit(solution)/shard_map/ppermute | solution.py:360
  (196 shorter events, 69.0 us)
Async XLA Ops:
  3.4 20.6 %all-to-all-start = ((bf16[8,512,128]{2,1,0:T(8,128)(2,1)}), bf16[8,512,128]{2,1,0:T(8,128)(2,1)S(1)}, u32[]{:S(2)}, u32[]{:S(2)}) async-start(bf16[8,512,128]{2,1,0:T(8,128)(2,1)} %broadcast_in_dim.28), calls=%async_computation | async-start | bytes 2097152 | tf_op jit(solution)/shard_map/all_to_all | solution.py:258
  9.5 15.0 %collective-permute-start = (bf16[4,128,256]{2,1,0:T(8,128)(2,1)S(1)}, bf16[4,128,256]{2,1,0:T(8,128)(2,1)S(1)}, u32[]{:S(2)}, u32[]{:S(2)}) collective-permute-start(bf16[4,128,256]{2,1,0:T(8,128)(2,1)S(1)} %get-tuple-element.52), channel_id=1, source_target_pairs={{0,1},{1,0},{2,3},{3,2},{4,5},{5,4},{6,7},{7,6},{8,9},{9,8},{10,11... | collective-permute-start | bytes 786440 | tf_op jit(solution)/shard_map/ppermute | solution.py:201
  24.0 33.3 %collective-permute-start.5 = (bf16[8,512,128]{2,1,0:T(8,128)(2,1)S(1)}, bf16[8,512,128]{2,1,0:T(8,128)(2,1)}, u32[]{:S(2)}, u32[]{:S(2)}) collective-permute-start(bf16[8,512,128]{2,1,0:T(8,128)(2,1)S(1)} %all-to-all-done), channel_id=1, source_target_pairs={{0,1},{1,0},{2,3},{3,2},{4,5},{5,4},{6,7},{7,6},{8,9},{9,8},{10,11... | collective-permute-start | bytes 3145736 | tf_op jit(solution)/shard_map/ppermute | solution.py:201
  24.0 62.4 %collective-permute-start.10 = (bf16[9,32,128]{2,1,0:T(8,128)(2,1)S(1)}, bf16[9,32,128]{2,1,0:T(8,128)(2,1)S(1)}, u32[]{:S(2)}, u32[]{:S(2)}) collective-permute-start(bf16[9,32,128]{2,1,0:T(8,128)(2,1)S(1)} %bitcast.51), channel_id=1, source_target_pairs={{0,1},{1,0},{2,3},{3,2},{4,5},{5,4},{6,7},{7,6},{8,9},{9,8},{10,11... | collective-permute-start | bytes 221192 | tf_op jit(solution)/shard_map/ppermute | solution.py:201
  24.6 27.7 %collective-permute-start.2 = (bf16[512,512]{1,0:T(8,128)(2,1)S(1)}, bf16[512,512]{1,0:T(8,128)(2,1)S(1)}, u32[]{:S(2)}, u32[]{:S(2)}) collective-permute-start(bf16[512,512]{1,0:T(8,128)(2,1)S(1)} %maximum_select_fusion.2.own.images), channel_id=1, source_target_pairs={{2,0},{3,1},{4,2},{5,3},{6,4},{7,5},{0,6},{1,7},{10,8},{11,9},{12,... | collective-permute-start | bytes 1572872 | tf_op jit(solution)/shard_map/ppermute | solution.py:215
  30.1 27.0 %collective-permute-start.1 = (bf16[512,512]{1,0:T(8,128)(2,1)S(1)}, bf16[512,512]{1,0:T(8,128)(2,1)S(1)}, u32[]{:S(2)}, u32[]{:S(2)}) collective-permute-start(bf16[512,512]{1,0:T(8,128)(2,1)S(1)} %maximum_select_fusion.2.own.images), channel_id=1, source_target_pairs={{0,2},{1,3},{2,4},{3,5},{4,6},{5,7},{6,0},{7,1},{8,10},{9,11},{10,... | collective-permute-start | bytes 1572872 | tf_op jit(solution)/shard_map/ppermute | solution.py:214
  52.4 15.2 %collective-permute-start.4 = (bf16[256,512]{1,0:T(8,128)(2,1)S(1)}, bf16[256,512]{1,0:T(8,128)(2,1)S(1)}, u32[]{:S(2)}, u32[]{:S(2)}) collective-permute-start(bf16[256,512]{1,0:T(8,128)(2,1)S(1)} %slice.185), channel_id=1, source_target_pairs={{2,0},{3,1},{4,2},{5,3},{6,4},{7,5},{0,6},{1,7},{10,8},{11,9},{12,... | collective-permute-start | bytes 786440 | tf_op jit(solution)/shard_map/ppermute | solution.py:217
  57.1 14.5 %collective-permute-start.3 = (bf16[256,512]{1,0:T(8,128)(2,1)S(1)}, bf16[256,512]{1,0:T(8,128)(2,1)S(1)}, u32[]{:S(2)}, u32[]{:S(2)}) collective-permute-start(bf16[256,512]{1,0:T(8,128)(2,1)S(1)} %slice.184), channel_id=1, source_target_pairs={{0,2},{1,3},{2,4},{3,5},{4,6},{5,7},{6,0},{7,1},{8,10},{9,11},{10,... | collective-permute-start | bytes 786440 | tf_op jit(solution)/shard_map/ppermute | solution.py:216
  80.6 15.1 %collective-permute-start.17 = (bf16[256,256]{1,0:T(8,128)(2,1)S(1)}, bf16[256,256]{1,0:T(8,128)(2,1)S(1)}, u32[]{:S(2)}, u32[]{:S(2)}) collective-permute-start(bf16[256,256]{1,0:T(8,128)(2,1)S(1)} %get-tuple-element.59), channel_id=1, source_target_pairs={{0,2},{1,3},{2,4},{3,5},{4,6},{5,7},{6,0},{7,1},{8,10},{9,11},{10,... | collective-permute-start | bytes 393224 | tf_op jit(solution)/shard_map/ppermute | solution.py:223
  82.7 12.2 %collective-permute-start.9 = (bf16[6,256]{1,0:T(8,128)(2,1)S(1)}, bf16[6,256]{1,0:T(8,128)(2,1)S(1)}, u32[]{:S(2)}, u32[]{:S(2)}) collective-permute-start(bf16[6,256]{1,0:T(8,128)(2,1)S(1)} %pad_maximum_fusion.4), channel_id=1, source_target_pairs={{1,0},{8,1},{3,2},{10,3},{5,4},{12,5},{7,6},{14,7},{9,8},{16,9},{1... | collective-permute-start | bytes 9224 | tf_op jit(solution)/shard_map/ppermute | solution.py:254
  86.6 18.0 %collective-permute-start.19 = (bf16[256,256]{1,0:T(8,128)(2,1)S(1)}, bf16[256,256]{1,0:T(8,128)(2,1)S(1)}, u32[]{:S(2)}, u32[]{:S(2)}) collective-permute-start(bf16[256,256]{1,0:T(8,128)(2,1)S(1)} %slice.160), channel_id=1, source_target_pairs={{2,0},{3,1},{4,2},{5,3},{6,4},{7,5},{0,6},{1,7},{10,8},{11,9},{12,... | collective-permute-start | bytes 393224 | tf_op jit(solution)/shard_map/ppermute | solution.py:224
  90.8 13.9 %collective-permute-start.20 = (bf16[256,256]{1,0:T(8,128)(2,1)S(1)}, bf16[256,256]{1,0:T(8,128)(2,1)S(1)}, u32[]{:S(2)}, u32[]{:S(2)}) collective-permute-start(bf16[256,256]{1,0:T(8,128)(2,1)S(1)} %slice.161), channel_id=1, source_target_pairs={{0,2},{1,3},{2,4},{3,5},{4,6},{5,7},{6,0},{7,1},{8,10},{9,11},{10,... | collective-permute-start | bytes 393224 | tf_op jit(solution)/shard_map/ppermute | solution.py:222
  122.9 13.2 %collective-permute-start.12 = (bf16[512,256]{1,0:T(8,128)(2,1)S(1)}, bf16[512,256]{1,0:T(8,128)(2,1)S(1)}, u32[]{:S(2)}, u32[]{:S(2)}) collective-permute-start(bf16[512,256]{1,0:T(8,128)(2,1)S(1)} %get-tuple-element.22.own), channel_id=1, source_target_pairs={{2,0},{3,1},{4,2},{5,3},{6,4},{7,5},{0,6},{1,7},{10,8},{11,9},{12,... | collective-permute-start | bytes 786440 | tf_op jit(solution)/shard_map/ppermute | solution.py:215
  127.6 14.5 %collective-permute-start.11 = (bf16[512,256]{1,0:T(8,128)(2,1)S(1)}, bf16[512,256]{1,0:T(8,128)(2,1)S(1)}, u32[]{:S(2)}, u32[]{:S(2)}) collective-permute-start(bf16[512,256]{1,0:T(8,128)(2,1)S(1)} %get-tuple-element.22.own), channel_id=1, source_target_pairs={{0,2},{1,3},{2,4},{3,5},{4,6},{5,7},{6,0},{7,1},{8,10},{9,11},{10,... | collective-permute-start | bytes 786440 | tf_op jit(solution)/shard_map/ppermute | solution.py:214
  132.2 21.9 %collective-permute-start.34 = (bf16[2048,128]{1,0:T(8,128)(2,1)}, bf16[2048,128]{1,0:T(8,128)(2,1)}, u32[]{:S(2)}, u32[]{:S(2)}) collective-permute-start(bf16[2048,128]{1,0:T(8,128)(2,1)} %constant_dynamic-slice_fusion.2), channel_id=1, source_target_pairs={{0,1},{1,0},{2,3},{3,2},{4,5},{5,4},{6,7},{7,6},{8,9},{9,8},{10,11... | collective-permute-start | bytes 1572872 | tf_op jit(solution)/shard_map/ppermute | solution.py:201
  157.7 62.6 %all-to-all-start.1 = ((bf16[8,800,128]{2,1,0:T(8,128)(2,1)}), bf16[8,800,128]{2,1,0:T(8,128)(2,1)S(1)}, u32[]{:S(2)}, u32[]{:S(2)}) async-start(bf16[8,800,128]{2,1,0:T(8,128)(2,1)} %pad_maximum_fusion), calls=%async_computation.1 | async-start | bytes 3276800 | tf_op jit(solution)/shard_map/all_to_all | solution.py:354
  166.7 36.3 %collective-permute-start.31 = (bf16[256,512]{1,0:T(8,128)(2,1)S(1)}, bf16[256,512]{1,0:T(8,128)(2,1)S(1)}, u32[]{:S(2)}, u32[]{:S(2)}) collective-permute-start(bf16[256,512]{1,0:T(8,128)(2,1)S(1)} %get-tuple-element.46), channel_id=1, source_target_pairs={{2,0},{3,1},{4,2},{5,3},{6,4},{7,5},{0,6},{1,7},{10,8},{11,9},{12,... | collective-permute-start | bytes 786440 | tf_op jit(solution)/shard_map/ppermute | solution.py:225
  170.9 37.8 %collective-permute-start.29 = (bf16[256,512]{1,0:T(8,128)(2,1)S(1)}, bf16[256,512]{1,0:T(8,128)(2,1)S(1)}, u32[]{:S(2)}, u32[]{:S(2)}) collective-permute-start(bf16[256,512]{1,0:T(8,128)(2,1)S(1)} %slice.174), channel_id=1, source_target_pairs={{2,0},{3,1},{4,2},{5,3},{6,4},{7,5},{0,6},{1,7},{10,8},{11,9},{12,... | collective-permute-start | bytes 786440 | tf_op jit(solution)/shard_map/ppermute | solution.py:224
  171.0 37.7 %collective-permute-start.30 = (bf16[256,512]{1,0:T(8,128)(2,1)S(1)}, bf16[256,512]{1,0:T(8,128)(2,1)S(1)}, u32[]{:S(2)}, u32[]{:S(2)}) collective-permute-start(bf16[256,512]{1,0:T(8,128)(2,1)S(1)} %slice.175), channel_id=1, source_target_pairs={{0,2},{1,3},{2,4},{3,5},{4,6},{5,7},{6,0},{7,1},{8,10},{9,11},{10,... | collective-permute-start | bytes 786440 | tf_op jit(solution)/shard_map/ppermute | solution.py:222
  178.2 30.4 %collective-permute-start.28 = (bf16[256,512]{1,0:T(8,128)(2,1)S(1)}, bf16[256,512]{1,0:T(8,128)(2,1)S(1)}, u32[]{:S(2)}, u32[]{:S(2)}) collective-permute-start(bf16[256,512]{1,0:T(8,128)(2,1)S(1)} %add_convert_fusion.3), channel_id=1, source_target_pairs={{0,2},{1,3},{2,4},{3,5},{4,6},{5,7},{6,0},{7,1},{8,10},{9,11},{10,... | collective-permute-start | bytes 786440 | tf_op jit(solution)/shard_map/ppermute | solution.py:226
  203.1 15.7 %collective-permute-start.32 = (bf16[256,512]{1,0:T(8,128)(2,1)S(1)}, bf16[256,512]{1,0:T(8,128)(2,1)S(1)}, u32[]{:S(2)}, u32[]{:S(2)}) collective-permute-start(bf16[256,512]{1,0:T(8,128)(2,1)S(1)} %add_convert_fusion.2), channel_id=1, source_target_pairs={{2,0},{3,1},{4,2},{5,3},{6,4},{7,5},{0,6},{1,7},{10,8},{11,9},{12,... | collective-permute-start | bytes 786440 | tf_op jit(solution)/shard_map/ppermute | solution.py:229
  220.6 12.7 %collective-permute-start.39 = (bf16[800,128]{1,0:T(8,128)(2,1)S(1)}, bf16[800,128]{1,0:T(8,128)(2,1)S(1)}, u32[]{:S(2)}, u32[]{:S(2)}) collective-permute-start(bf16[800,128]{1,0:T(8,128)(2,1)S(1)} %reduce_sum.12), channel_id=1, source_target_pairs={{64,0},{128,64},{192,128},{0,192},{65,1},{129,65},{193,129},{1,193... | collective-permute-start | bytes 614408 | tf_op jit(solution)/shard_map/ppermute | solution.py:360
  223.9 12.8 %collective-permute-start.38 = (bf16[800,128]{1,0:T(8,128)(2,1)S(1)}, bf16[800,128]{1,0:T(8,128)(2,1)S(1)}, u32[]{:S(2)}, u32[]{:S(2)}) collective-permute-start(bf16[800,128]{1,0:T(8,128)(2,1)S(1)} %reduce_sum.12), channel_id=1, source_target_pairs={{0,64},{64,128},{128,192},{192,0},{1,65},{65,129},{129,193},{193,1... | collective-permute-start | bytes 614408 | tf_op jit(solution)/shard_map/ppermute | solution.py:359
  223.9 12.8 %collective-permute-start.37 = (bf16[800,128]{1,0:T(8,128)(2,1)S(1)}, bf16[800,128]{1,0:T(8,128)(2,1)S(1)}, u32[]{:S(2)}, u32[]{:S(2)}) collective-permute-start(bf16[800,128]{1,0:T(8,128)(2,1)S(1)} %reduce_sum.12), channel_id=1, source_target_pairs={{0,128},{64,192},{128,0},{192,64},{1,129},{65,193},{129,1},{193,65... | collective-permute-start | bytes 614408 | tf_op jit(solution)/shard_map/ppermute | solution.py:361
  (44 other events, 448.5 us)

commit v2 on v0

v2 whole, which is shorter than its diff:
```python
import jax
import jax.numpy as jnp
from jax import lax
from jax.experimental import pallas as pl
from jax.experimental.pallas import tpu as pltpu
from jax.sharding import PartitionSpec as P

F32 = jnp.float32
BF16 = jnp.bfloat16
VMEM = pl.BlockSpec(memory_space=pltpu.VMEM)
SMEM = pl.BlockSpec(memory_space=pltpu.SMEM)


def dot(a, b, ca=1, cb=0):
    return lax.dot_general(a, b, (((ca,), (cb,)), ((), ())), preferred_element_type=F32)


def call(kernel, outs, args, scratch=(), after=()):
    def ordered(*refs):
        kernel(*refs[: len(args)], *refs[len(args) + len(after) :])

    return pl.pallas_call(
        ordered,
        out_shape=[jax.ShapeDtypeStruct(s, d) for s, d in outs],
        in_specs=[SMEM]
        + [VMEM] * (len(args) - 1)
        + [pl.BlockSpec(memory_space=pl.ANY)] * len(after),
        out_specs=[VMEM] * len(outs),
        scratch_shapes=list(scratch),
        compiler_params=pltpu.CompilerParams(vmem_limit_bytes=48 * 2**20),
    )(*args, *after)


def span(index, size):
    return pl.ds(pl.multiple_of(index * size, size), size)


def logistic(v):
    return 1.0 / (1.0 + jnp.exp(-v))


def slope(v):
    s = logistic(v)
    return s * (1.0 + v * (1.0 - s))


def split_kernel(place, images, grad, own, send):
    core = lax.rem(place[0], 2)
    rows, cols = images.shape[0], images.shape[1] // 2
    for i, x in enumerate((images, grad)):
        for r in range(rows):
            at = slice(r * cols, (r + 1) * cols)
            own[i, at, :] = x[r, span(core, cols), :]
            send[i, at, :] = x[r, span(1 - core, cols), :]


def join_kernel(place, own, got, images, grad):
    for i, out in enumerate((images, grad)):
        out[0] = own[i]
        out[1] = got[i]


def gather_kernel(place, a0, a1, a2, a3, b0, b1, b2, b3, taps, taps_other, w1, w3, wd):
    core, chan = lax.rem(place[0], 2), place[2]
    low_z, y_here = lax.rem(chan, 2), chan // 2
    depth, half = w1.shape[1], a0.shape[2]
    mine, theirs = (a0, a1, a2, a3), (b0, b1, b2, b3)

    def fill(low, high, low_taps, high_taps):
        for step in range(4):
            y = y_here ^ step
            for s in range(2):
                k = 2 * y + (low_z ^ s)
                w1[k, :, :half] = low[step][s, :depth, :]
                w1[k, :, half:] = high[step][s, :depth, :]
                rows = span(low_z ^ s, half)
                for slot, refs in enumerate((mine, theirs)):
                    for i in range(2):
                        lanes = slice(i * half, (i + 1) * half)
                        at = slice(depth + i * half, depth + (i + 1) * half)
                        w3[y, slot, rows, lanes] = refs[step][s, at, :]
        chans = wd.shape[1]
        size = taps.shape[0] // 9
        row_group = lax.broadcasted_iota(jnp.int32, (chans, chans), 0) // size
        col_group = lax.broadcasted_iota(jnp.int32, (chans, chans), 1) // size
        keep = row_group == col_group
        both = jnp.concatenate([low_taps[...], high_taps[...]], axis=1).astype(F32)
        for t in range(9):
            whole = jnp.concatenate([both[t * size : (t + 1) * size]] * (chans // size), axis=0)
            wd[t] = jnp.where(keep, whole, 0.0).astype(BF16)

    @pl.when(core == 0)
    def _():
        fill(mine, theirs, taps, taps_other)

    @pl.when(core == 1)
    def _():
        fill(theirs, mine, taps_other, taps)


def block(place, step, slot):
    zone = lax.rem(place[0] // 2 + step, 4)
    return 2 * zone + (lax.rem(place[0], 2) ^ slot)


def outline(v, cols, top, bottom, first, last):
    rows = v.shape[0] // cols
    top[...] = v[:cols].astype(BF16)
    bottom[...] = v[(rows - 1) * cols :].astype(BF16)
    for out, c in ((first, 0), (last, cols - 1)):
        lines = [v[r * cols + c : r * cols + c + 1] for r in range(rows)]
        pad = jnp.zeros((out.shape[0] - rows - 1, v.shape[1]), F32)
        out[...] = jnp.concatenate([pad[:1]] + lines + [pad], axis=0).astype(BF16)


def first_kernel(place, own, left, right, far_a, far_b, w1, pre, act, top, bottom, first, last):
    total = None
    for step, slots in ((0, own), (3, left), (1, right), (2, (far_a, far_b))):
        for s in range(2):
            x = slots[s][...] if step == 2 else slots[s]
            v = dot(x, w1[block(place, step, s)])
            total = v if total is None else total + v
    pre[...] = total
    a = total * logistic(total)
    act[...] = a.astype(BF16)
    outline(a, top.shape[0], top, bottom, first, last)


def shifted(up, mid, down, low, high, out):
    cols, chans = up.shape
    n = mid.shape[0] + 2 * cols
    x = jnp.concatenate([up[...].astype(F32), mid[...].astype(F32), down[...].astype(F32)], axis=0)
    col = lax.rem(lax.broadcasted_iota(jnp.int32, (n, chans), 0), cols)

    def spread(edge):
        e = edge[...].astype(F32)
        parts = [jnp.broadcast_to(e[i : i + 1, :], (cols, chans)) for i in range(n // cols)]
        return jnp.concatenate(parts, axis=0)

    out[1] = x.astype(BF16)
    out[0] = jnp.where(col == 0, spread(low), pltpu.roll(x, 1, 0)).astype(BF16)
    out[2] = jnp.where(col == cols - 1, spread(high), pltpu.roll(x, n - 1, 0)).astype(BF16)


def group_kernel(place, up, mid, down, low, high, wd, pre, act, xs):
    n, cols = mid.shape[0], up.shape[0]
    shifted(up, mid, down, low, high, xs)
    total = None
    for a in range(3):
        for b in range(3):
            v = dot(xs[b, a * cols : a * cols + n, :], wd[3 * a + b])
            total = v if total is None else total + v
    pre[...] = total
    act[...] = (total * logistic(total)).astype(BF16)


def mid_kernel(place, grad, w3, p0, p1, p2a, p2b, p3):
    zone = place[0] // 2

    def part(step):
        z = lax.rem(zone + step, 4)
        return dot(grad[0], w3[z, 0], 1, 1) + dot(grad[1], w3[z, 1], 1, 1)

    half = p2a.shape[0]
    far = part(2).astype(BF16)
    p2a[...] = far[:half]
    p2b[...] = far[half:]
    p1[...] = part(1).astype(BF16)
    p3[...] = part(3).astype(BF16)
    p0[...] = part(0)


def pass_kernel(place, p1, p3, got_a, got_b, plus, minus):
    half = got_a.shape[0]
    plus[:half, :] = (p1[:half, :].astype(F32) + got_a[...].astype(F32)).astype(BF16)
    plus[half:, :] = p1[half:, :]
    minus[:half, :] = p3[:half, :]
    minus[half:, :] = (p3[half:, :].astype(F32) + got_b[...].astype(F32)).astype(BF16)


def delta_kernel(place, p0, plus, minus, pre, delta, top, bottom, first, last):
    mid = p0[...] + plus[...].astype(F32) + minus[...].astype(F32)
    d = mid * slope(pre[...])
    delta[...] = d.astype(BF16)
    outline(d, top.shape[0], top, bottom, first, last)


def back_kernel(place, up, mid, down, low, high, wd, pre, w1, fdelta, p0, p1, p2a, p2b, p3, ds):
    n, cols = mid.shape[0], up.shape[0]
    shifted(up, mid, down, low, high, ds)
    total = None
    for a in range(3):
        for b in range(3):
            at = (2 - a) * cols
            v = dot(ds[2 - b, at : at + n, :], wd[3 * a + b], 1, 1)
            total = v if total is None else total + v
    d = (total * slope(pre[...])).astype(BF16)
    fdelta[...] = d
    for s, out in ((0, p2a), (1, p2b)):
        out[...] = dot(d, w1[block(place, 2, s)], 1, 1).astype(BF16)
    for step, out in ((1, p1), (3, p3), (0, p0)):
        for s in range(2):
            v = dot(d, w1[block(place, step, s)], 1, 1)
            out[s * n : (s + 1) * n, :] = v.astype(out.dtype)


def combine_kernel(place, p0, plus, minus, keep, send):
    n = keep.shape[0]
    for s, out in ((0, keep), (1, send)):
        at = slice(s * n, (s + 1) * n)
        v = p0[at, :] + plus[at, :].astype(F32) + minus[at, :].astype(F32)
        out[...] = v.astype(out.dtype)


def merge_kernel(place, keep, got, out):
    core = lax.rem(place[0], 2)
    rows, cols = out.shape[0], out.shape[1] // 2
    for r in range(rows):
        at = slice(r * cols, (r + 1) * cols)
        out[r, span(core, cols), :] = keep[at, :]
        out[r, span(1 - core, cols), :] = got[at, :]


def merge_add_kernel(place, base, keep, got, out):
    core = lax.rem(place[0], 2)
    rows, cols = out.shape[0], out.shape[1] // 2
    for r in range(rows):
        at = slice(r * cols, (r + 1) * cols)
        for there, piece in ((span(core, cols), keep), (span(1 - core, cols), got)):
            out[r, there, :] = base[r, there, :].astype(F32) + piece[at, :].astype(F32)


def third_kernel(
    place, own, left, right, far_a, far_b, w3, grad, images, out_keep, out_send, keep, send
):
    zone = place[0] // 2
    acts = (
        (0, own[...]),
        (3, left[...]),
        (1, right[...]),
        (2, jnp.concatenate([far_a[...], far_b[...]], axis=0)),
    )
    for s, out in ((0, out_keep), (1, out_send)):
        total = images[s].astype(F32)
        third = None
        for step, a in acts:
            v = dot(a, w3[lax.rem(zone + step, 4), s])
            third = v if third is None else third + v
        out[...] = (total + third).astype(BF16)
    for step, a in acts:
        z = lax.rem(zone + step, 4)
        at = a.astype(F32).T.astype(BF16)
        size = at.shape[0]
        keep[span(z, size), :] = dot(at, grad[0])
        send[span(z, size), :] = dot(at, grad[1]).astype(BF16)


def group_grad_kernel(place, xs, delta, keep_out, send_out):
    core = lax.rem(place[0], 2)
    n, chans = delta.shape
    cols = (xs.shape[1] - n) // 2
    size = keep_out.shape[0] * 2 // 9
    wide = chans // 2
    d = delta[...]
    row_group = lax.broadcasted_iota(jnp.int32, (chans, chans), 0) // size
    col_group = lax.broadcasted_iota(jnp.int32, (chans, chans), 1) // size
    diag = row_group == col_group
    taps = []
    for t in range(9):
        a, b = t // 3, t % 3
        full = jnp.where(diag, dot(xs[b, a * cols : a * cols + n, :], d, 0, 0), 0.0)
        total = full[0:size]
        for g in range(1, chans // size):
            total += full[g * size : (g + 1) * size]
        taps.append(total)
    both = jnp.concatenate(taps, axis=0)
    half = both.shape[0] // 2
    low = jnp.concatenate([both[:half, :wide], both[half:, :wide]], axis=1)
    high = jnp.concatenate([both[:half, wide:], both[half:, wide:]], axis=1)
    keep_out[...] = jnp.where(core == 0, low, high)
    send_out[...] = jnp.where(core == 0, high, low).astype(BF16)


def first_grad_kernel(
    place, own, left, right, far_a, far_b, delta, group_keep, group_send, keep, send
):
    core = lax.rem(place[0], 2)
    d = delta[...].astype(F32).T.astype(BF16)
    rows = d.shape[0] // 2
    for step, slots in ((0, own), (3, left), (1, right), (2, (far_a, far_b))):
        for s in range(2):
            v = dot(d, slots[s][...] if step == 2 else slots[s])
            low, high = v[:rows], v[rows:]
            at = span(block(place, step, s), rows)
            keep[at, :] = jnp.where(core == 0, low, high)
            send[at, :] = jnp.where(core == 0, high, low).astype(BF16)
    keep[8 * rows :, :] = group_keep[...]
    send[8 * rows :, :] = group_send[...]


def pack_kernel(place, keep, got, third_keep, third_got, o0, o1, o2, o3):
    low_z, y_here = lax.rem(place[2], 2), place[2] // 2
    rows = third_keep.shape[0] // 8
    group = keep.shape[0] - 8 * rows
    part = (keep[8 * rows :, :] + got[8 * rows :, :].astype(F32)).astype(BF16)
    for step, out in enumerate((o0, o1, o2, o3)):
        for s in range(2):
            at = span(2 * (y_here ^ step) + (low_z ^ s), rows)
            out[s, :rows, :] = (keep[at, :] + got[at, :].astype(F32)).astype(BF16)
            out[s, rows : rows + group, :] = part
            v = third_keep[at, :] + third_got[at, :].astype(F32)
            out[s, rows + group :, :] = v.astype(BF16)


def sum_kernel(place, a, b, c, d, keep, send):
    for s, out in ((0, keep), (1, send)):
        v = (a[s].astype(F32) + c[s].astype(F32)) + (b[s].astype(F32) + d[s].astype(F32))
        out[...] = v.astype(out.dtype)


def add_kernel(place, keep, got, out):
    out[...] = (keep[...] + got[...].astype(F32)).astype(BF16)


def last_kernel(place, own, a, b, c, first, group, third):
    total = (own[...].astype(F32) + b[...].astype(F32)) + (
        a[...].astype(F32) + c[...].astype(F32)
    )
    wide = first.shape[1]
    half = group.shape[0] // 2
    first[...] = total[:wide].T
    group[:half, :] = total[wide : wide + half, :wide]
    group[half:, :] = total[wide : wide + half, wide:]
    third[...] = total[wide + half :]


def body(images, first_weight, group_weight, third_weight, out_grad):
    rows_here, cols_here, chans = images.shape
    filt, chan, rows = lax.axis_size("filt"), lax.axis_size("chan"), lax.axis_size("rows")
    zones = filt // 2
    place = jnp.stack([lax.axis_index(a) for a in ("filt", "rows", "chan")]).astype(jnp.int32)
    cols = cols_here // 2
    n = rows_here * cols
    depth, own_mid = first_weight.shape
    hidden = 2 * own_mid
    pair = (2, n, chans)

    def xor(axis, k):
        return [(i, i ^ k) for i in range(lax.axis_size(axis))]

    zplus = [(z * 2 + c, (z + 1) % zones * 2 + c) for z in range(zones) for c in range(2)]
    zminus = [(t, s) for s, t in zplus]
    row_next = [(i, i + 1) for i in range(rows - 1)]
    row_prev = [(t, s) for s, t in row_next]
    col_next = [
        (k * filt + 2 * z + c, k * filt + 2 * z + 1 if c == 0 else (k + 1) * filt + 2 * z)
        for k in range(chan)
        for z in range(zones)
        for c in range(2)
        if c == 0 or k < chan - 1
    ]
    col_prev = [(t, s) for s, t in col_next]

    def swap(v):
        return lax.ppermute(v, "filt", xor("filt", 1))

    def up_z(v):
        return lax.ppermute(v, "filt", zplus)

    def down_z(v):
        return lax.ppermute(v, "filt", zminus)

    def along_y(pieces):
        return [pieces[0]] + [
            lax.ppermute(pieces[k], "chan", xor("chan", 2 * k)) for k in range(1, 4)
        ]

    def ring_scatter(p0, p1, p2a, p2b, p3, after=()):
        shape = p1.shape
        plus, minus = call(
            pass_kernel,
            [(shape, BF16)] * 2,
            (place, p1, p3, up_z(p2a), down_z(p2b)),
            after=after,
        )
        return (p0, up_z(plus), down_z(minus)), plus

    def halo(v, top, bottom, first, last):
        up = lax.ppermute(bottom, "rows", row_next)
        down = lax.ppermute(top, "rows", row_prev)

        def line(edge, c):
            end = slice(c, c + 1)
            return jnp.concatenate(
                [up[end], edge[1 : rows_here + 1], down[end], edge[rows_here + 2 :]], axis=0
            )

        low = lax.ppermute(line(last, cols - 1), ("chan", "filt"), col_next)
        high = lax.ppermute(line(first, 0), ("chan", "filt"), col_prev)
        return up, v, down, low, high

    panel = jnp.concatenate(
        [first_weight] + [third_weight[:, i : i + own_mid] for i in range(0, chans, own_mid)],
        axis=0,
    )
    taps = group_weight.reshape(-1, own_mid)
    beside = lax.ppermute(panel, "chan", xor("chan", 1))

    own, send = call(split_kernel, [(pair, BF16)] * 2, (place, images, out_grad))
    img, grad = call(
        join_kernel, [(pair, BF16)] * 2, (place, own, swap(send)), after=(beside,)
    )
    left, right = up_z(img), down_z(img)
    blocks = (img, left, right, up_z(left[0]), down_z(right[1]))

    panel = jnp.stack([panel, beside])
    panels = along_y([panel] * 4)
    w1, w3, wd = call(
        gather_kernel,
        [
            ((chan, depth, hidden), BF16),
            ((zones, 2, hidden, chans), BF16),
            ((9, hidden, hidden), BF16),
        ],
        (place, *panels, *[swap(p) for p in panels], taps, swap(taps)),
    )

    flat = (n, hidden)
    half = (n // 2, hidden)
    mid_parts = call(
        mid_kernel,
        [(flat, F32), (flat, BF16), (half, BF16), (half, BF16), (flat, BF16)],
        (place, grad, w3),
    )
    mid_parts, passed = ring_scatter(*mid_parts)
    around = [((cols, hidden), BF16)] * 2 + [((16, hidden), BF16)] * 2
    pre_first, act_first, *edge = call(
        first_kernel,
        [(flat, F32), (flat, BF16)] + around,
        (place, *blocks, w1),
        after=(passed,),
    )
    pre_group, act_group, xs = call(
        group_kernel,
        [(flat, F32), (flat, BF16), ((3, n + 2 * cols, hidden), BF16)],
        (place, *halo(act_first, *edge), wd),
    )
    act_left, act_right = up_z(act_group), down_z(act_group)
    delta, *edge = call(
        delta_kernel, [(flat, BF16)] + around, (place, *mid_parts, pre_group)
    )
    acts = (
        act_group,
        act_left,
        act_right,
        up_z(act_left[: n // 2]),
        down_z(act_right[n // 2 :]),
    )
    two = (2 * n, chans)
    first_delta, *back_parts = call(
        back_kernel,
        [(flat, BF16), (two, F32), (two, BF16)] + [((n, chans), BF16)] * 2 + [(two, BF16)],
        (place, *halo(delta, *edge), wd, pre_first, w1),
        [pltpu.VMEM((3, n + 2 * cols, hidden), BF16)],
        after=(act_left, act_right),
    )
    group_keep, group_send = call(
        group_grad_kernel,
        [((taps.shape[0] // 2, hidden), F32), ((taps.shape[0] // 2, hidden), BF16)],
        (place, xs, delta),
    )

    out_keep, out_send, third_keep, third_send = call(
        third_kernel,
        [((n, chans), BF16)] * 2
        + [((chan * own_mid, chans), F32), ((chan * own_mid, chans), BF16)],
        (place, *acts, w3, grad, img),
        after=(first_delta,),
    )
    (block_out,) = call(
        merge_kernel, [(images.shape, BF16)], (place, out_keep, swap(out_send))
    )

    lines = own_mid + taps.shape[0] // 2
    keep, send = call(
        first_grad_kernel,
        [((lines + (chan - 1) * own_mid, chans), d) for d in (F32, BF16)],
        (place, *blocks, first_delta, group_keep, group_send),
    )
    back_parts, passed = ring_scatter(*back_parts, after=(keep, third_keep))
    lines += own_mid
    pieces = call(
        pack_kernel,
        [((2, lines, chans), BF16)] * 4,
        (place, keep, swap(send), third_keep, swap(third_send)),
    )
    keep, send = call(
        sum_kernel,
        [((lines, chans), F32), ((lines, chans), BF16)],
        (place, *along_y(pieces)),
    )
    (total,) = call(
        add_kernel,
        [((lines, chans), BF16)],
        (place, keep, lax.ppermute(send, "chan", xor("chan", 1))),
    )
    others = [lax.ppermute(total, "rows", xor("rows", k)) for k in range(1, 4)]
    first_grad, group_grad, third_grad = call(
        last_kernel,
        [((depth, own_mid), F32), (taps.shape, F32), ((own_mid, chans), F32)],
        (place, total, *others),
    )

    keep, send = call(
        combine_kernel, [((n, chans), F32), ((n, chans), BF16)], (place, *back_parts)
    )
    (images_grad,) = call(
        merge_add_kernel, [(images.shape, F32)], (place, out_grad, keep, swap(send))
    )
    return (block_out, images_grad, first_grad, group_grad.reshape(group_weight.shape), third_grad)


def solution(mesh):
    in_specs = (
        P("rows", "chan", "filt"),
        P("chan", "filt"),
        P(None, None, None, "filt"),
        P("chan", "filt"),
        P("rows", "chan", "filt"),
    )
    out_specs = (
        P("rows", "chan", "filt"),
        P("rows", "chan", "filt"),
        P("chan", "filt"),
        P(None, None, None, "filt"),
        P("chan", "filt"),
    )
    return jax.shard_map(body, mesh=mesh, in_specs=in_specs, out_specs=out_specs, check_vma=False)
```

time: 701 us -> 189 us (0.27)
  waiting for transfers between devices: 487 us -> 81.6 us
  blocking collectives: 76.5 us -> 0 us
  starting transfers between devices: 22 us -> 77.1 us
  matrix products: 49 us -> 0 us
  local copies, waits for them, and re-layouts: 43.4 us -> 3.02 us
  Pallas kernels: 0 us -> 23.7 us
  between operations: 14.5 us -> 1.09 us
  other arithmetic: 7.29 us -> 0.18 us
    psum x2 -> x0, waiting for transfers between devices: 312 us -> none  [the longest x1 291 us: body(): group_grad = lax.psum(kernel_part, ('rows', 'chan'))]
    reduce_scatter x4 -> x0, waiting for transfers between devices: 144 us -> none  [the longest x1 59.3 us: body(): lax.psum_scatter(input_terms.reshape(rows_here, cols_here, input_terms.sh...]
    all_gather x2 -> x0, blocking collectives: 76.5 us -> none  [the longest x1 39.6 us: body(): lax.all_gather(third_weight, 'chan', axis=0, tiled=True)]
    ppermute x8 -> x45, starting transfers between devices: 21.4 us -> 77.1 us  [the longest x8 20.3 us: down_z(): return lax.ppermute(v, 'filt', zminus)]
    ppermute x8 -> x45, waiting for transfers between devices: 30.6 us -> 81.6 us  [the longest x8 42.7 us: up_z(): return lax.ppermute(v, 'filt', zplus)]
    dot_general x15 -> x0, matrix products: 25.7 us -> none  [the longest x1 4.41 us: body(): jnp.dot(flat_images, first_panel, preferred_element_type=jnp.float32)]
    pallas_call x0 -> x20, Pallas kernels: none -> 23.7 us  [call(): pl.pallas_call(ordered, out_shape=[jax.ShapeDtypeStruct(s, d) for s, d in...]
    conv_general_dilated x2 -> x0, matrix products: 23.3 us -> none  [group_conv(): lax.conv_general_dilated(padded[None], kernel, (1, 1), 'VALID', dimension...]
  transfers between devices with their start and end apart: 16 -> 45, of which waited for: 12 -> 18; matrix products, arithmetic and copies ran while one was open for 13% -> 1% of each run, Pallas kernels for 0% -> 10%
where the time goes in v2:
time: 189 us; the launch traced here: 187 us
  waiting for transfers between devices  81.6 us (43%)
  starting transfers between devices  77.1 us (41%)
  Pallas kernels  23.7 us (13%)
  local copies, waits for them, and re-layouts  3.02 us (2%)
    ppermute x8, waiting for transfers between devices, up_z(): return lax.ppermute(v, 'filt', zplus)  42.7 us
    pallas_call x20, Pallas kernels, call(): pl.pallas_call(ordered, out_shape=[jax.ShapeDtypeStruct(s, d) for s, d in...  23.7 us
    ppermute x8, starting transfers between devices, down_z(): return lax.ppermute(v, 'filt', zminus)  20.3 us
    ppermute x8, starting transfers between devices, up_z(): return lax.ppermute(v, 'filt', zplus)  14.1 us
    ppermute x2, waiting for transfers between devices, halo(): down = lax.ppermute(top, 'rows', row_prev)  9.67 us
    ppermute x6, starting transfers between devices, along_y(): lax.ppermute(pieces[k], 'chan', xor('chan', 2 * k))  9.57 us
    ppermute x6, waiting for transfers between devices, along_y(): lax.ppermute(pieces[k], 'chan', xor('chan', 2 * k))  8.49 us
    ppermute x2, starting transfers between devices, halo(): high = lax.ppermute(line(first, 0), ('chan', 'filt'), col_prev)  7.85 us
  transfers between devices with their start and end apart: 45, of which 18 were waited for; matrix products, arithmetic and copies ran while one was open for 1% of the time, Pallas kernels for 10%

profile of v2, /device:TPU:32, one launch (start us, length us, event | category | flops | bytes accessed | tf_op | source)
XLA Modules:
  0.0 186.6 jit_solution(5910143986516651633)
XLA Ops:
  6.3 4.2 %collective-permute-done.1.refs_3_ = bf16[512,128]{1,0:T(8,128)(2,1)S(1)} collective-permute-done((bf16[512,128]{1,0:T(8,128)(2,1)S(1)}, bf16[512,128]{1,0:T(8,128)(2,1)S(1)}, u32[]{:S(2)}, u32[]{:S(2)}) %collective-permute-start.1) | collective-permute-done | bytes 131104 | tf_op jit(solution)/shard_map/ppermute | solution.py:407
  11.1 3.2 %collective-permute-start.2 = (bf16[2,512,256]{2,1,0:T(8,128)(2,1)S(1)}, bf16[2,512,256]{2,1,0:T(8,128)(2,1)S(1)}, u32[]{:S(2)}, u32[]{:S(2)}) collective-permute-start(bf16[2,512,256]{2,1,0:T(8,128)(2,1)S(1)} %get-tuple-element.62.refs_1_.refs_8_), channel_id=1, source_target_pairs={{0,2},{1,3},{2,4},{3,5},{4,6},{5,7},{6,0},{7,1},{8,10},{9,11},{10,... | collective-permute-start | bytes 1572872 | tf_op jit(solution)/shard_map/ppermute | solution.py:368
  18.2 2.9 %collective-permute-start.7 = (bf16[2,512,128]{2,1,0:T(8,128)(2,1)S(1)}, bf16[2,512,128]{2,1,0:T(8,128)(2,1)S(1)}, u32[]{:S(2)}, u32[]{:S(2)}) collective-permute-start(bf16[2,512,128]{2,1,0:T(8,128)(2,1)S(1)} %pad_maximum_fusion.refs_1_), channel_id=1, source_target_pairs={{0,32},{8,40},{16,48},{24,56},{32,0},{40,8},{48,16},{56,24},{1,33}... | collective-permute-start | bytes 786440 | tf_op jit(solution)/shard_map/ppermute | solution.py:375
  21.3 18.1 %collective-permute-done.2.refs_2_ = bf16[2,512,256]{2,1,0:T(8,128)(2,1)S(1)} collective-permute-done((bf16[2,512,256]{2,1,0:T(8,128)(2,1)S(1)}, bf16[2,512,256]{2,1,0:T(8,128)(2,1)S(1)}, u32[]{:S(2)}, u32[]{:S(2)}) %collective-permute-start.2) | collective-permute-done | bytes 524320 | tf_op jit(solution)/shard_map/ppermute | solution.py:368
  41.1 3.0 %collective-permute-start.4 = (bf16[512,256]{1,0:T(8,128)(2,1)S(1)}, bf16[512,256]{1,0:T(8,128)(2,1)S(1)}, u32[]{:S(2)}, u32[]{:S(2)}) collective-permute-start(bf16[512,256]{1,0:T(8,128)(2,1)S(1)} %slice_bitcast_fusion.1), channel_id=1, source_target_pairs={{0,2},{1,3},{2,4},{3,5},{4,6},{5,7},{6,0},{7,1},{8,10},{9,11},{10,... | collective-permute-start | bytes 786440 | tf_op jit(solution)/shard_map/ppermute | solution.py:368
  51.9 7.8 %collective-permute-done.14.refs_3_ = bf16[256,256]{1,0:T(8,128)(2,1)S(1)} collective-permute-done((bf16[256,256]{1,0:T(8,128)(2,1)S(1)}, bf16[256,256]{1,0:T(8,128)(2,1)S(1)}, u32[]{:S(2)}, u32[]{:S(2)}) %collective-permute-start.14) | collective-permute-done | bytes 131104 | tf_op jit(solution)/shard_map/ppermute | solution.py:368
  61.6 3.4 %collective-permute-start.16 = (bf16[128,256]{1,0:T(8,128)(2,1)S(1)}, bf16[128,256]{1,0:T(8,128)(2,1)S(1)}, u32[]{:S(2)}, u32[]{:S(2)}) collective-permute-start(bf16[128,256]{1,0:T(8,128)(2,1)S(1)} %get-tuple-element.71), channel_id=1, source_target_pairs={{0,64},{64,128},{128,192},{1,65},{65,129},{129,193},{2,66},{66,130... | collective-permute-start | bytes 196616 | tf_op jit(solution)/shard_map/ppermute | solution.py:389
  70.6 4.8 %collective-permute-done.17.refs_3_ = bf16[128,256]{1,0:T(8,128)(2,1)S(1)} collective-permute-done((bf16[128,256]{1,0:T(8,128)(2,1)S(1)}, bf16[128,256]{1,0:T(8,128)(2,1)S(1)}, u32[]{:S(2)}, u32[]{:S(2)}) %collective-permute-start.17) | collective-permute-done | bytes 65568 | tf_op jit(solution)/shard_map/ppermute | solution.py:390
  75.5 5.9 %collective-permute-start.19 = (bf16[16,256]{1,0:T(8,128)(2,1)S(1)}, bf16[16,256]{1,0:T(8,128)(2,1)S(1)}, u32[]{:S(2)}, u32[]{:S(2)}) collective-permute-start(bf16[16,256]{1,0:T(8,128)(2,1)S(1)} %pad_maximum_fusion.3), channel_id=1, source_target_pairs={{1,0},{8,1},{3,2},{10,3},{5,4},{12,5},{7,6},{14,7},{9,8},{16,9},{1... | collective-permute-start | bytes 24584 | tf_op jit(solution)/shard_map/ppermute | solution.py:399
  83.4 3.7 %collective-permute-done.18.refs_4_ = bf16[16,256]{1,0:T(8,128)(2,1)S(1)} collective-permute-done((bf16[16,256]{1,0:T(8,128)(2,1)S(1)}, bf16[16,256]{1,0:T(8,128)(2,1)S(1)}, u32[]{:S(2)}, u32[]{:S(2)}) %collective-permute-start.18) | collective-permute-done | bytes 8224 | tf_op jit(solution)/shard_map/ppermute | solution.py:398
  89.3 3.4 %collective-permute-start.26 = (bf16[128,256]{1,0:T(8,128)(2,1)S(1)}, bf16[128,256]{1,0:T(8,128)(2,1)S(1)}, u32[]{:S(2)}, u32[]{:S(2)}) collective-permute-start(bf16[128,256]{1,0:T(8,128)(2,1)S(1)} %get-tuple-element.81), channel_id=1, source_target_pairs={{0,64},{64,128},{128,192},{1,65},{65,129},{129,193},{2,66},{66,130... | collective-permute-start | bytes 196616 | tf_op jit(solution)/shard_map/ppermute | solution.py:389
  93.6 3.4 %collective-permute-start.21 = (bf16[512,256]{1,0:T(8,128)(2,1)S(1)}, bf16[512,256]{1,0:T(8,128)(2,1)S(1)}, u32[]{:S(2)}, u32[]{:S(2)}) collective-permute-start(bf16[512,256]{1,0:T(8,128)(2,1)S(1)} %get-tuple-element.77.refs_1_), channel_id=1, source_target_pairs={{2,0},{3,1},{4,2},{5,3},{6,4},{7,5},{0,6},{1,7},{10,8},{11,9},{12,... | collective-permute-start | bytes 786440 | tf_op jit(solution)/shard_map/ppermute | solution.py:371
  98.3 4.8 %collective-permute-done.27.refs_3_ = bf16[128,256]{1,0:T(8,128)(2,1)S(1)} collective-permute-done((bf16[128,256]{1,0:T(8,128)(2,1)S(1)}, bf16[128,256]{1,0:T(8,128)(2,1)S(1)}, u32[]{:S(2)}, u32[]{:S(2)}) %collective-permute-start.27) | collective-permute-done | bytes 65568 | tf_op jit(solution)/shard_map/ppermute | solution.py:390
  108.3 3.0 %collective-permute-start.23 = (bf16[256,256]{1,0:T(8,128)(2,1)S(1)}, bf16[256,256]{1,0:T(8,128)(2,1)S(1)}, u32[]{:S(2)}, u32[]{:S(2)}) collective-permute-start(bf16[256,256]{1,0:T(8,128)(2,1)S(1)} %slice.95), channel_id=1, source_target_pairs={{2,0},{3,1},{4,2},{5,3},{6,4},{7,5},{0,6},{1,7},{10,8},{11,9},{12,... | collective-permute-start | bytes 393224 | tf_op jit(solution)/shard_map/ppermute | solution.py:371
  116.3 3.7 %shard_map.100 = (bf16[512,256]{1,0:T(8,128)(2,1)S(1)}, f32[1024,256]{1,0:T(8,128)S(1)}, bf16[1024,256]{1,0:T(8,128)(2,1)S(1)}, bf16[512,256]{1,0:T(8,128)(2,1)S...) custom-call(s32[3]{0:T(128)S(1)} %pad_add_fusion.refs_0_, ...), custom_call_target="tpu_custom_call" | custom-call | tf_op jit(solution)/shard_map/pallas_call | solution.py:22
  125.0 4.1 %collective-permute-start.32 = (bf16[512,256]{1,0:T(8,128)(2,1)S(1)}, bf16[512,256]{1,0:T(8,128)(2,1)S(1)}, u32[]{:S(2)}, u32[]{:S(2)}) collective-permute-start(bf16[512,256]{1,0:T(8,128)(2,1)S(1)} %get-tuple-element.94), channel_id=1, source_target_pairs={{2,0},{3,1},{4,2},{5,3},{6,4},{7,5},{0,6},{1,7},{10,8},{11,9},{12,... | collective-permute-start | bytes 786440 | tf_op jit(solution)/shard_map/ppermute | solution.py:371
  134.7 5.5 %collective-permute-done.31.refs_3_ = bf16[512,256]{1,0:T(8,128)(2,1)S(1)} collective-permute-done((bf16[512,256]{1,0:T(8,128)(2,1)S(1)}, bf16[512,256]{1,0:T(8,128)(2,1)S(1)}, u32[]{:S(2)}, u32[]{:S(2)}) %collective-permute-start.31) | collective-permute-done | bytes 262176 | tf_op jit(solution)/shard_map/ppermute | solution.py:368
  145.0 5.9 %collective-permute-done.39.refs_3_ = bf16[2,400,256]{2,1,0:T(8,128)(2,1)S(1)} collective-permute-done((bf16[2,400,256]{2,1,0:T(8,128)(2,1)S(1)}, bf16[2,400,256]{2,1,0:T(8,128)(2,1)S(1)}, u32[]{:S(2)}, u32[]{:S(2)}) %collective-permute-start.39) | collective-permute-done | bytes 409632 | tf_op jit(solution)/shard_map/ppermute | solution.py:375
  150.9 2.6 %collective-permute-done.40.refs_4_ = bf16[2,400,256]{2,1,0:T(8,128)(2,1)S(1)} collective-permute-done((bf16[2,400,256]{2,1,0:T(8,128)(2,1)S(1)}, bf16[2,400,256]{2,1,0:T(8,128)(2,1)S(1)}, u32[]{:S(2)}, u32[]{:S(2)}) %collective-permute-start.40) | collective-permute-done | bytes 409632 | tf_op jit(solution)/shard_map/ppermute | solution.py:375
  156.5 9.3 %collective-permute-done.33.refs_2_ = bf16[1024,256]{1,0:T(8,128)(2,1)S(1)} collective-permute-done((bf16[1024,256]{1,0:T(8,128)(2,1)S(1)}, bf16[1024,256]{1,0:T(8,128)(2,1)S(1)}, u32[]{:S(2)}, u32[]{:S(2)}) %collective-permute-start.33) | collective-permute-done | bytes 524320 | tf_op jit(solution)/shard_map/ppermute | solution.py:368
  165.7 2.9 %collective-permute-done.34.refs_3_ = bf16[1024,256]{1,0:T(8,128)(2,1)S(1)} collective-permute-done((bf16[1024,256]{1,0:T(8,128)(2,1)S(1)}, bf16[1024,256]{1,0:T(8,128)(2,1)S(1)}, u32[]{:S(2)}, u32[]{:S(2)}) %collective-permute-start.34) | collective-permute-done | bytes 524320 | tf_op jit(solution)/shard_map/ppermute | solution.py:371
  169.4 2.8 %collective-permute-done.41.refs_2_ = bf16[400,256]{1,0:T(8,128)(2,1)S(1)} collective-permute-done((bf16[400,256]{1,0:T(8,128)(2,1)S(1)}, bf16[400,256]{1,0:T(8,128)(2,1)S(1)}, u32[]{:S(2)}, u32[]{:S(2)}) %collective-permute-start.41) | collective-permute-done | bytes 204832 | tf_op jit(solution)/shard_map/ppermute | solution.py:505
  174.4 3.2 %collective-permute-start.44 = (bf16[400,256]{1,0:T(8,128)(2,1)S(1)}, bf16[400,256]{1,0:T(8,128)(2,1)S(1)}, u32[]{:S(2)}, u32[]{:S(2)}) collective-permute-start(bf16[400,256]{1,0:T(8,128)(2,1)S(1)} %shard_map.110.refs_1_), channel_id=1, source_target_pairs={{0,192},{64,128},{128,64},{192,0},{1,193},{65,129},{129,65},{193,1... | collective-permute-start | bytes 614408 | tf_op jit(solution)/shard_map/ppermute | solution.py:507
  182.6 2.7 %collective-permute-done.44.refs_4_ = bf16[400,256]{1,0:T(8,128)(2,1)S(1)} collective-permute-done((bf16[400,256]{1,0:T(8,128)(2,1)S(1)}, bf16[400,256]{1,0:T(8,128)(2,1)S(1)}, u32[]{:S(2)}, u32[]{:S(2)}) %collective-permute-start.44) | collective-permute-done | bytes 204832 | tf_op jit(solution)/shard_map/ppermute | solution.py:507
  (122 shorter events, 71.1 us)
Async XLA Ops:
  11.1 28.4 %collective-permute-start.2 = (bf16[2,512,256]{2,1,0:T(8,128)(2,1)S(1)}, bf16[2,512,256]{2,1,0:T(8,128)(2,1)S(1)}, u32[]{:S(2)}, u32[]{:S(2)}) collective-permute-start(bf16[2,512,256]{2,1,0:T(8,128)(2,1)S(1)} %get-tuple-element.62.refs_1_.refs_8_), channel_id=1, source_target_pairs={{0,2},{1,3},{2,4},{3,5},{4,6},{5,7},{6,0},{7,1},{8,10},{9,11},{10,... | collective-permute-start | bytes 1572872 | tf_op jit(solution)/shard_map/ppermute | solution.py:368
  14.3 26.3 %collective-permute-start.3 = (bf16[2,512,256]{2,1,0:T(8,128)(2,1)S(1)}, bf16[2,512,256]{2,1,0:T(8,128)(2,1)S(1)}, u32[]{:S(2)}, u32[]{:S(2)}) collective-permute-start(bf16[2,512,256]{2,1,0:T(8,128)(2,1)S(1)} %get-tuple-element.62.refs_1_.refs_8_), channel_id=1, source_target_pairs={{2,0},{3,1},{4,2},{5,3},{6,4},{7,5},{0,6},{1,7},{10,8},{11,9},{12,... | collective-permute-start | bytes 1572872 | tf_op jit(solution)/shard_map/ppermute | solution.py:371
  16.5 22.9 %collective-permute-start.6 = (bf16[2,512,128]{2,1,0:T(8,128)(2,1)S(1)}, bf16[2,512,128]{2,1,0:T(8,128)(2,1)S(1)}, u32[]{:S(2)}, u32[]{:S(2)}) collective-permute-start(bf16[2,512,128]{2,1,0:T(8,128)(2,1)S(1)} %pad_maximum_fusion.refs_1_), channel_id=1, source_target_pairs={{0,16},{8,24},{16,0},{24,8},{32,48},{40,56},{48,32},{56,40},{1,17}... | collective-permute-start | bytes 786440 | tf_op jit(solution)/shard_map/ppermute | solution.py:375
  18.2 21.9 %collective-permute-start.7 = (bf16[2,512,128]{2,1,0:T(8,128)(2,1)S(1)}, bf16[2,512,128]{2,1,0:T(8,128)(2,1)S(1)}, u32[]{:S(2)}, u32[]{:S(2)}) collective-permute-start(bf16[2,512,128]{2,1,0:T(8,128)(2,1)S(1)} %pad_maximum_fusion.refs_1_), channel_id=1, source_target_pairs={{0,32},{8,40},{16,48},{24,56},{32,0},{40,8},{48,16},{56,24},{1,33}... | collective-permute-start | bytes 786440 | tf_op jit(solution)/shard_map/ppermute | solution.py:375
  21.1 19.1 %collective-permute-start.8 = (bf16[2,512,128]{2,1,0:T(8,128)(2,1)S(1)}, bf16[2,512,128]{2,1,0:T(8,128)(2,1)S(1)}, u32[]{:S(2)}, u32[]{:S(2)}) collective-permute-start(bf16[2,512,128]{2,1,0:T(8,128)(2,1)S(1)} %pad_maximum_fusion.refs_1_), channel_id=1, source_target_pairs={{0,48},{8,56},{16,32},{24,40},{32,16},{40,24},{48,0},{56,8},{1,49}... | collective-permute-start | bytes 786440 | tf_op jit(solution)/shard_map/ppermute | solution.py:375
  41.1 19.2 %collective-permute-start.4 = (bf16[512,256]{1,0:T(8,128)(2,1)S(1)}, bf16[512,256]{1,0:T(8,128)(2,1)S(1)}, u32[]{:S(2)}, u32[]{:S(2)}) collective-permute-start(bf16[512,256]{1,0:T(8,128)(2,1)S(1)} %slice_bitcast_fusion.1), channel_id=1, source_target_pairs={{0,2},{1,3},{2,4},{3,5},{4,6},{5,7},{6,0},{7,1},{8,10},{9,11},{10,... | collective-permute-start | bytes 786440 | tf_op jit(solution)/shard_map/ppermute | solution.py:368
  44.2 16.2 %collective-permute-start.5 = (bf16[512,256]{1,0:T(8,128)(2,1)S(1)}, bf16[512,256]{1,0:T(8,128)(2,1)S(1)}, u32[]{:S(2)}, u32[]{:S(2)}) collective-permute-start(bf16[512,256]{1,0:T(8,128)(2,1)S(1)} %slice_bitcast_fusion), channel_id=1, source_target_pairs={{2,0},{3,1},{4,2},{5,3},{6,4},{7,5},{0,6},{1,7},{10,8},{11,9},{12,... | collective-permute-start | bytes 786440 | tf_op jit(solution)/shard_map/ppermute | solution.py:371
  47.7 12.0 %collective-permute-start.14 = (bf16[256,256]{1,0:T(8,128)(2,1)S(1)}, bf16[256,256]{1,0:T(8,128)(2,1)S(1)}, u32[]{:S(2)}, u32[]{:S(2)}) collective-permute-start(bf16[256,256]{1,0:T(8,128)(2,1)S(1)} %get-tuple-element.68), channel_id=1, source_target_pairs={{0,2},{1,3},{2,4},{3,5},{4,6},{5,7},{6,0},{7,1},{8,10},{9,11},{10,... | collective-permute-start | bytes 393224 | tf_op jit(solution)/shard_map/ppermute | solution.py:368
  65.0 23.4 %collective-permute-start.24 = (bf16[512,256]{1,0:T(8,128)(2,1)S(1)}, bf16[512,256]{1,0:T(8,128)(2,1)S(1)}, u32[]{:S(2)}, u32[]{:S(2)}) collective-permute-start(bf16[512,256]{1,0:T(8,128)(2,1)S(1)} %get-tuple-element.70.refs_7_), channel_id=1, source_target_pairs={{0,2},{1,3},{2,4},{3,5},{4,6},{5,7},{6,0},{7,1},{8,10},{9,11},{10,... | collective-permute-start | bytes 786440 | tf_op jit(solution)/shard_map/ppermute | solution.py:368
  67.2 21.3 %collective-permute-start.25 = (bf16[512,256]{1,0:T(8,128)(2,1)S(1)}, bf16[512,256]{1,0:T(8,128)(2,1)S(1)}, u32[]{:S(2)}, u32[]{:S(2)}) collective-permute-start(bf16[512,256]{1,0:T(8,128)(2,1)S(1)} %get-tuple-element.79), channel_id=1, source_target_pairs={{2,0},{3,1},{4,2},{5,3},{6,4},{7,5},{0,6},{1,7},{10,8},{11,9},{12,... | collective-permute-start | bytes 786440 | tf_op jit(solution)/shard_map/ppermute | solution.py:371
  92.7 14.3 %collective-permute-start.20 = (bf16[512,256]{1,0:T(8,128)(2,1)S(1)}, bf16[512,256]{1,0:T(8,128)(2,1)S(1)}, u32[]{:S(2)}, u32[]{:S(2)}) collective-permute-start(bf16[512,256]{1,0:T(8,128)(2,1)S(1)} %get-tuple-element.77.refs_1_), channel_id=1, source_target_pairs={{0,2},{1,3},{2,4},{3,5},{4,6},{5,7},{6,0},{7,1},{8,10},{9,11},{10,... | collective-permute-start | bytes 786440 | tf_op jit(solution)/shard_map/ppermute | solution.py:368
  93.6 14.7 %collective-permute-start.21 = (bf16[512,256]{1,0:T(8,128)(2,1)S(1)}, bf16[512,256]{1,0:T(8,128)(2,1)S(1)}, u32[]{:S(2)}, u32[]{:S(2)}) collective-permute-start(bf16[512,256]{1,0:T(8,128)(2,1)S(1)} %get-tuple-element.77.refs_1_), channel_id=1, source_target_pairs={{2,0},{3,1},{4,2},{5,3},{6,4},{7,5},{0,6},{1,7},{10,8},{11,9},{12,... | collective-permute-start | bytes 786440 | tf_op jit(solution)/shard_map/ppermute | solution.py:371
  103.1 11.6 %collective-permute-start.29 = (bf16[16,256]{1,0:T(8,128)(2,1)S(1)}, bf16[16,256]{1,0:T(8,128)(2,1)S(1)}, u32[]{:S(2)}, u32[]{:S(2)}) collective-permute-start(bf16[16,256]{1,0:T(8,128)(2,1)S(1)} %pad_maximum_fusion.5), channel_id=1, source_target_pairs={{1,0},{8,1},{3,2},{10,3},{5,4},{12,5},{7,6},{14,7},{9,8},{16,9},{1... | collective-permute-start | bytes 24584 | tf_op jit(solution)/shard_map/ppermute | solution.py:399
  107.0 15.7 %collective-permute-start.22 = (bf16[256,256]{1,0:T(8,128)(2,1)S(1)}, bf16[256,256]{1,0:T(8,128)(2,1)S(1)}, u32[]{:S(2)}, u32[]{:S(2)}) collective-permute-start(bf16[256,256]{1,0:T(8,128)(2,1)S(1)} %slice.94), channel_id=1, source_target_pairs={{0,2},{1,3},{2,4},{3,5},{4,6},{5,7},{6,0},{7,1},{8,10},{9,11},{10,... | collective-permute-start | bytes 393224 | tf_op jit(solution)/shard_map/ppermute | solution.py:368
  108.3 14.5 %collective-permute-start.23 = (bf16[256,256]{1,0:T(8,128)(2,1)S(1)}, bf16[256,256]{1,0:T(8,128)(2,1)S(1)}, u32[]{:S(2)}, u32[]{:S(2)}) collective-permute-start(bf16[256,256]{1,0:T(8,128)(2,1)S(1)} %slice.95), channel_id=1, source_target_pairs={{2,0},{3,1},{4,2},{5,3},{6,4},{7,5},{0,6},{1,7},{10,8},{11,9},{12,... | collective-permute-start | bytes 393224 | tf_op jit(solution)/shard_map/ppermute | solution.py:371
  124.9 15.2 %collective-permute-start.31 = (bf16[512,256]{1,0:T(8,128)(2,1)S(1)}, bf16[512,256]{1,0:T(8,128)(2,1)S(1)}, u32[]{:S(2)}, u32[]{:S(2)}) collective-permute-start(bf16[512,256]{1,0:T(8,128)(2,1)S(1)} %get-tuple-element.93), channel_id=1, source_target_pairs={{0,2},{1,3},{2,4},{3,5},{4,6},{5,7},{6,0},{7,1},{8,10},{9,11},{10,... | collective-permute-start | bytes 786440 | tf_op jit(solution)/shard_map/ppermute | solution.py:368
  125.0 15.1 %collective-permute-start.32 = (bf16[512,256]{1,0:T(8,128)(2,1)S(1)}, bf16[512,256]{1,0:T(8,128)(2,1)S(1)}, u32[]{:S(2)}, u32[]{:S(2)}) collective-permute-start(bf16[512,256]{1,0:T(8,128)(2,1)S(1)} %get-tuple-element.94), channel_id=1, source_target_pairs={{2,0},{3,1},{4,2},{5,3},{6,4},{7,5},{0,6},{1,7},{10,8},{11,9},{12,... | collective-permute-start | bytes 786440 | tf_op jit(solution)/shard_map/ppermute | solution.py:371
  129.9 15.2 %collective-permute-start.38 = (bf16[2,400,256]{2,1,0:T(8,128)(2,1)S(1)}, bf16[2,400,256]{2,1,0:T(8,128)(2,1)S(1)}, u32[]{:S(2)}, u32[]{:S(2)}) collective-permute-start(bf16[2,400,256]{2,1,0:T(8,128)(2,1)S(1)} %get-tuple-element.107), channel_id=1, source_target_pairs={{0,16},{8,24},{16,0},{24,8},{32,48},{40,56},{48,32},{56,40},{1,17}... | collective-permute-start | bytes 1228808 | tf_op jit(solution)/shard_map/ppermute | solution.py:375
  131.5 19.5 %collective-permute-start.39 = (bf16[2,400,256]{2,1,0:T(8,128)(2,1)S(1)}, bf16[2,400,256]{2,1,0:T(8,128)(2,1)S(1)}, u32[]{:S(2)}, u32[]{:S(2)}) collective-permute-start(bf16[2,400,256]{2,1,0:T(8,128)(2,1)S(1)} %get-tuple-element.108), channel_id=1, source_target_pairs={{0,32},{8,40},{16,48},{24,56},{32,0},{40,8},{48,16},{56,24},{1,33}... | collective-permute-start | bytes 1228808 | tf_op jit(solution)/shard_map/ppermute | solution.py:375
  133.2 20.3 %collective-permute-start.40 = (bf16[2,400,256]{2,1,0:T(8,128)(2,1)S(1)}, bf16[2,400,256]{2,1,0:T(8,128)(2,1)S(1)}, u32[]{:S(2)}, u32[]{:S(2)}) collective-permute-start(bf16[2,400,256]{2,1,0:T(8,128)(2,1)S(1)} %get-tuple-element.109), channel_id=1, source_target_pairs={{0,48},{8,56},{16,32},{24,40},{32,16},{40,24},{48,0},{56,8},{1,49}... | collective-permute-start | bytes 1228808 | tf_op jit(solution)/shard_map/ppermute | solution.py:375
  140.8 24.9 %collective-permute-start.33 = (bf16[1024,256]{1,0:T(8,128)(2,1)S(1)}, bf16[1024,256]{1,0:T(8,128)(2,1)S(1)}, u32[]{:S(2)}, u32[]{:S(2)}) collective-permute-start(bf16[1024,256]{1,0:T(8,128)(2,1)S(1)} %get-tuple-element.100), channel_id=1, source_target_pairs={{0,2},{1,3},{2,4},{3,5},{4,6},{5,7},{6,0},{7,1},{8,10},{9,11},{10,... | collective-permute-start | bytes 1572872 | tf_op jit(solution)/shard_map/ppermute | solution.py:368
  143.0 25.6 %collective-permute-start.34 = (bf16[1024,256]{1,0:T(8,128)(2,1)S(1)}, bf16[1024,256]{1,0:T(8,128)(2,1)S(1)}, u32[]{:S(2)}, u32[]{:S(2)}) collective-permute-start(bf16[1024,256]{1,0:T(8,128)(2,1)S(1)} %get-tuple-element.101), channel_id=1, source_target_pairs={{2,0},{3,1},{4,2},{5,3},{6,4},{7,5},{0,6},{1,7},{10,8},{11,9},{12,... | collective-permute-start | bytes 1572872 | tf_op jit(solution)/shard_map/ppermute | solution.py:371
  154.3 18.0 %collective-permute-start.41 = (bf16[400,256]{1,0:T(8,128)(2,1)S(1)}, bf16[400,256]{1,0:T(8,128)(2,1)S(1)}, u32[]{:S(2)}, u32[]{:S(2)}) collective-permute-start(bf16[400,256]{1,0:T(8,128)(2,1)S(1)} %get-tuple-element.111), channel_id=1, source_target_pairs={{0,8},{8,0},{16,24},{24,16},{32,40},{40,32},{48,56},{56,48},{1,9},... | collective-permute-start | bytes 614408 | tf_op jit(solution)/shard_map/ppermute | solution.py:505
  156.5 21.2 %collective-permute-start.30 = (bf16[512,256]{1,0:T(8,128)(2,1)S(1)}, bf16[512,256]{1,0:T(8,128)(2,1)S(1)}, u32[]{:S(2)}, u32[]{:S(2)}) collective-permute-start(bf16[512,256]{1,0:T(8,128)(2,1)S(1)} %get-tuple-element.89), channel_id=1, source_target_pairs={{0,1},{1,0},{2,3},{3,2},{4,5},{5,4},{6,7},{7,6},{8,9},{9,8},{10,11... | collective-permute-start | bytes 786440 | tf_op jit(solution)/shard_map/ppermute | solution.py:365
  (27 other events, 231.2 us)

commit v3 on v2

--- a/solution.py
+++ b/solution.py
@@ -19,16 +19,22 @@
     def ordered(*refs):
         kernel(*refs[: len(args)], *refs[len(args) + len(after) :])
 
-    return pl.pallas_call(
-        ordered,
-        out_shape=[jax.ShapeDtypeStruct(s, d) for s, d in outs],
-        in_specs=[SMEM]
-        + [VMEM] * (len(args) - 1)
-        + [pl.BlockSpec(memory_space=pl.ANY)] * len(after),
-        out_specs=[VMEM] * len(outs),
-        scratch_shapes=list(scratch),
-        compiler_params=pltpu.CompilerParams(vmem_limit_bytes=48 * 2**20),
-    )(*args, *after)
+    weight = WEIGHT.get(kernel.__name__, 1)
+    with jax.named_scope(kernel.__name__):
+        return pl.pallas_call(
+            ordered,
+            out_shape=[jax.ShapeDtypeStruct(s, d) for s, d in outs],
+            in_specs=[SMEM]
+            + [VMEM] * (len(args) - 1)
+            + [pl.BlockSpec(memory_space=pl.ANY)] * len(after),
+            out_specs=[VMEM] * len(outs),
+            scratch_shapes=list(scratch),
+            cost_estimate=pl.CostEstimate(flops=weight, bytes_accessed=weight, transcendentals=0),
+            compiler_params=pltpu.CompilerParams(vmem_limit_bytes=48 * 2**20),
+        )(*args, *after)
+
+
+WEIGHT = {"back_kernel": 3 * 10**10}
 
 
 def span(index, size):
@@ -58,6 +64,15 @@
     for i, out in enumerate((images, grad)):
         out[0] = own[i]
         out[1] = got[i]
+
+
+def panel_kernel(place, first, third, first_got, third_got, out):
+    depth, wide = first.shape
+    for s, (a, b) in enumerate(((first, third), (first_got, third_got))):
+        out[s, :depth, :] = a[...]
+        for i in range(b.shape[1] // wide):
+            at = slice(depth + i * b.shape[0], depth + (i + 1) * b.shape[0])
+            out[s, at, :] = b[:, i * wide : (i + 1) * wide]
 
 
 def gather_kernel(place, a0, a1, a2, a3, b0, b1, b2, b3, taps, taps_other, w1, w3, wd):
@@ -301,37 +316,38 @@
 def pack_kernel(place, keep, got, third_keep, third_got, o0, o1, o2, o3):
     low_z, y_here = lax.rem(place[2], 2), place[2] // 2
     rows = third_keep.shape[0] // 8
-    group = keep.shape[0] - 8 * rows
     part = (keep[8 * rows :, :] + got[8 * rows :, :].astype(F32)).astype(BF16)
     for step, out in enumerate((o0, o1, o2, o3)):
         for s in range(2):
             at = span(2 * (y_here ^ step) + (low_z ^ s), rows)
-            out[s, :rows, :] = (keep[at, :] + got[at, :].astype(F32)).astype(BF16)
-            out[s, rows : rows + group, :] = part
+            v = keep[at, :] + got[at, :].astype(F32)
+            out[2 * s * rows : (2 * s + 1) * rows, :] = v.astype(BF16)
             v = third_keep[at, :] + third_got[at, :].astype(F32)
-            out[s, rows + group :, :] = v.astype(BF16)
+            out[(2 * s + 1) * rows : (2 * s + 2) * rows, :] = v.astype(BF16)
+        out[4 * rows :, :] = part
+
+
+def sum_y_kernel(place, a, b, c, d, out):
+    v = (a[...].astype(F32) + c[...].astype(F32)) + (b[...].astype(F32) + d[...].astype(F32))
+    out[...] = v.astype(BF16)
 
 
 def sum_kernel(place, a, b, c, d, keep, send):
-    for s, out in ((0, keep), (1, send)):
-        v = (a[s].astype(F32) + c[s].astype(F32)) + (b[s].astype(F32) + d[s].astype(F32))
-        out[...] = v.astype(out.dtype)
-
-
-def add_kernel(place, keep, got, out):
-    out[...] = (keep[...] + got[...].astype(F32)).astype(BF16)
-
-
-def last_kernel(place, own, a, b, c, first, group, third):
-    total = (own[...].astype(F32) + b[...].astype(F32)) + (
-        a[...].astype(F32) + c[...].astype(F32)
-    )
+    v = (a[...].astype(F32) + c[...].astype(F32)) + (b[...].astype(F32) + d[...].astype(F32))
+    keep[...] = v[: keep.shape[0]]
+    send[...] = v[keep.shape[0] :].astype(BF16)
+
+
+def last_kernel(place, keep, send, got, first, group, third):
+    mine = keep.shape[0]
     wide = first.shape[1]
+    total = keep[...] + got[:mine, :].astype(F32)
+    first[...] = total[:wide].T
+    third[...] = total[wide:]
+    part = send[mine:, :].astype(F32) + got[mine:, :].astype(F32)
     half = group.shape[0] // 2
-    first[...] = total[:wide].T
-    group[:half, :] = total[wide : wide + half, :wide]
-    group[half:, :] = total[wide : wide + half, wide:]
-    third[...] = total[wide + half :]
+    group[:half, :] = part[:, :wide]
+    group[half:, :] = part[:, wide:]
 
 
 def body(images, first_weight, group_weight, third_weight, out_grad):
@@ -399,21 +415,22 @@
         high = lax.ppermute(line(first, 0), ("chan", "filt"), col_prev)
         return up, v, down, low, high
 
-    panel = jnp.concatenate(
-        [first_weight] + [third_weight[:, i : i + own_mid] for i in range(0, chans, own_mid)],
-        axis=0,
-    )
     taps = group_weight.reshape(-1, own_mid)
-    beside = lax.ppermute(panel, "chan", xor("chan", 1))
+    beside = [lax.ppermute(w, "chan", xor("chan", 1)) for w in (first_weight, third_weight)]
 
     own, send = call(split_kernel, [(pair, BF16)] * 2, (place, images, out_grad))
     img, grad = call(
-        join_kernel, [(pair, BF16)] * 2, (place, own, swap(send)), after=(beside,)
+        join_kernel, [(pair, BF16)] * 2, (place, own, swap(send)), after=beside
     )
     left, right = up_z(img), down_z(img)
     blocks = (img, left, right, up_z(left[0]), down_z(right[1]))
 
-    panel = jnp.stack([panel, beside])
+    (panel,) = call(
+        panel_kernel,
+        [((2, depth + third_weight.size // own_mid, own_mid), BF16)],
+        (place, first_weight, third_weight, *beside),
+        after=(img,),
+    )
     panels = along_y([panel] * 4)
     w1, w3, wd = call(
         gather_kernel,
@@ -438,12 +455,12 @@
         first_kernel,
         [(flat, F32), (flat, BF16)] + around,
         (place, *blocks, w1),
-        after=(passed,),
     )
     pre_group, act_group, xs = call(
         group_kernel,
         [(flat, F32), (flat, BF16), ((3, n + 2 * cols, hidden), BF16)],
         (place, *halo(act_first, *edge), wd),
+        after=(passed,),
     )
     act_left, act_right = up_z(act_group), down_z(act_group)
     delta, *edge = call(
@@ -491,24 +508,21 @@
     lines += own_mid
     pieces = call(
         pack_kernel,
-        [((2, lines, chans), BF16)] * 4,
+        [((lines + 2 * own_mid, chans), BF16)] * 4,
         (place, keep, swap(send), third_keep, swap(third_send)),
     )
+    lined = [((lines + 2 * own_mid, chans), BF16)]
+    (total,) = call(sum_y_kernel, lined, (place, *along_y(pieces)))
+    others = [lax.ppermute(total, "rows", xor("rows", k)) for k in range(1, 4)]
     keep, send = call(
         sum_kernel,
-        [((lines, chans), F32), ((lines, chans), BF16)],
-        (place, *along_y(pieces)),
-    )
-    (total,) = call(
-        add_kernel,
-        [((lines, chans), BF16)],
-        (place, keep, lax.ppermute(send, "chan", xor("chan", 1))),
-    )
-    others = [lax.ppermute(total, "rows", xor("rows", k)) for k in range(1, 4)]
+        [((2 * own_mid, chans), F32), ((lines, chans), BF16)],
+        (place, total, *others),
+    )
     first_grad, group_grad, third_grad = call(
         last_kernel,
         [((depth, own_mid), F32), (taps.shape, F32), ((own_mid, chans), F32)],
-        (place, total, *others),
+        (place, keep, send, lax.ppermute(send, "chan", xor("chan", 1))),
     )
 
     keep, send = call(

time: 189 us -> 174 us (0.921)
  waiting for transfers between devices: 81.6 us -> 64.8 us
  starting transfers between devices: 77.1 us -> 79.8 us
    ppermute x8, waiting for transfers between devices: 42.7 us -> 34.8 us  [up_z(): return lax.ppermute(v, 'filt', zplus)]
    ppermute x8, starting transfers between devices: 14.1 us -> 18.7 us  [up_z(): return lax.ppermute(v, 'filt', zplus)]
    ppermute x6, waiting for transfers between devices: 8.49 us -> 5.36 us  [along_y(): lax.ppermute(pieces[k], 'chan', xor('chan', 2 * k))]
    ppermute x3, waiting for transfers between devices: 4.66 us -> 2.56 us  [body(): others = [lax.ppermute(total, 'rows', xor('rows', k)) for k in range(1, 4)]]
    pallas_call x20 -> x21, Pallas kernels: 23.7 us -> 24.4 us  [call(): pl.pallas_call(ordered, out_shape=[jax.ShapeDtypeStruct(s, d) for s, d in...]
    ppermute x1 -> x2, waiting for transfers between devices: 4.16 us -> 4.29 us  [body(): lax.ppermute(w, 'chan', xor('chan', 1))]
  transfers between devices with their start and end apart: 45 -> 46, of which waited for: 18 -> 16; matrix products, arithmetic and copies ran while one was open for 1% -> 0% of each run, Pallas kernels for 10% -> 12%
where the time goes in v3:
time: 174 us; the launch traced here: 172 us
  starting transfers between devices  79.8 us (46%)
  waiting for transfers between devices  64.8 us (37%)
  Pallas kernels  24.4 us (14%)
  local copies, waits for them, and re-layouts  2.24 us (1%)
    ppermute x8, waiting for transfers between devices, up_z(): return lax.ppermute(v, 'filt', zplus)  34.8 us
    pallas_call x21, Pallas kernels, call(): pl.pallas_call(ordered, out_shape=[jax.ShapeDtypeStruct(s, d) for s, d in...  24.4 us
    ppermute x8, starting transfers between devices, up_z(): return lax.ppermute(v, 'filt', zplus)  18.7 us
    ppermute x8, starting transfers between devices, down_z(): return lax.ppermute(v, 'filt', zminus)  18.5 us
    ppermute x2, waiting for transfers between devices, halo(): down = lax.ppermute(top, 'rows', row_prev)  9.67 us
    ppermute x6, starting transfers between devices, along_y(): lax.ppermute(pieces[k], 'chan', xor('chan', 2 * k))  9.57 us
    ppermute x2, starting transfers between devices, halo(): high = lax.ppermute(line(first, 0), ('chan', 'filt'), col_prev)  7.22 us
    ppermute x2, starting transfers between devices, halo(): up = lax.ppermute(bottom, 'rows', row_next)  6.79 us
  transfers between devices with their start and end apart: 46, of which 16 were waited for; matrix products, arithmetic and copies ran while one was open for 0% of the time, Pallas kernels for 12%

profile of v3, /device:TPU:32, one launch (start us, length us, event | category | flops | bytes accessed | tf_op | source)
XLA Modules:
  0.0 172.4 jit_solution(16758523168047301565)
XLA Ops:
  5.6 2.7 %collective-permute-done.1.refs_3_ = bf16[256,128]{1,0:T(8,128)(2,1)S(1)} collective-permute-done((bf16[256,128]{1,0:T(8,128)(2,1)}, bf16[256,128]{1,0:T(8,128)(2,1)S(1)}, u32[]{:S(2)}, u32[]{:S(2)}) %collective-permute-start.1) | collective-permute-done | bytes 65568 | tf_op jit(solution)/shard_map/ppermute | solution.py:419
  10.6 3.1 %collective-permute-start.3 = (bf16[2,512,256]{2,1,0:T(8,128)(2,1)S(1)}, bf16[2,512,256]{2,1,0:T(8,128)(2,1)S(1)}, u32[]{:S(2)}, u32[]{:S(2)}) collective-permute-start(bf16[2,512,256]{2,1,0:T(8,128)(2,1)S(1)} %get-tuple-element.62.refs_5_.refs_1_.refs_8_), channel_id=1, source_target_pairs={{0,2},{1,3},{2,4},{3,5},{4,6},{5,7},{6,0},{7,1},{8,10},{9,11},{10,... | collective-permute-start | bytes 1572872 | tf_op jit(solution)/shard_map/ppermute | solution.py:384
  18.1 2.9 %collective-permute-start.8 = (bf16[2,512,128]{2,1,0:T(8,128)(2,1)S(1)}, bf16[2,512,128]{2,1,0:T(8,128)(2,1)S(1)}, u32[]{:S(2)}, u32[]{:S(2)}) collective-permute-start(bf16[2,512,128]{2,1,0:T(8,128)(2,1)S(1)} %panel_kernel.1.refs_1_), channel_id=1, source_target_pairs={{0,32},{8,40},{16,48},{24,56},{32,0},{40,8},{48,16},{56,24},{1,33}... | collective-permute-start | bytes 786440 | tf_op jit(solution)/shard_map/ppermute | solution.py:391
  21.2 17.5 %collective-permute-done.3.refs_2_ = bf16[2,512,256]{2,1,0:T(8,128)(2,1)S(1)} collective-permute-done((bf16[2,512,256]{2,1,0:T(8,128)(2,1)S(1)}, bf16[2,512,256]{2,1,0:T(8,128)(2,1)S(1)}, u32[]{:S(2)}, u32[]{:S(2)}) %collective-permute-start.3) | collective-permute-done | bytes 524320 | tf_op jit(solution)/shard_map/ppermute | solution.py:384
  40.4 3.0 %collective-permute-start.5 = (bf16[512,256]{1,0:T(8,128)(2,1)S(1)}, bf16[512,256]{1,0:T(8,128)(2,1)S(1)}, u32[]{:S(2)}, u32[]{:S(2)}) collective-permute-start(bf16[512,256]{1,0:T(8,128)(2,1)S(1)} %slice_bitcast_fusion.1), channel_id=1, source_target_pairs={{0,2},{1,3},{2,4},{3,5},{4,6},{5,7},{6,0},{7,1},{8,10},{9,11},{10,... | collective-permute-start | bytes 786440 | tf_op jit(solution)/shard_map/ppermute | solution.py:384
  51.2 2.9 %collective-permute-done.5.refs_4_ = bf16[512,256]{1,0:T(8,128)(2,1)S(1)} collective-permute-done((bf16[512,256]{1,0:T(8,128)(2,1)S(1)}, bf16[512,256]{1,0:T(8,128)(2,1)S(1)}, u32[]{:S(2)}, u32[]{:S(2)}) %collective-permute-start.5) | collective-permute-done | bytes 262176 | tf_op jit(solution)/shard_map/ppermute | solution.py:384
  55.7 3.4 %collective-permute-start.15 = (bf16[128,256]{1,0:T(8,128)(2,1)S(1)}, bf16[128,256]{1,0:T(8,128)(2,1)S(1)}, u32[]{:S(2)}, u32[]{:S(2)}) collective-permute-start(bf16[128,256]{1,0:T(8,128)(2,1)S(1)} %get-tuple-element.64), channel_id=1, source_target_pairs={{0,64},{64,128},{128,192},{1,65},{65,129},{129,193},{2,66},{66,130... | collective-permute-start | bytes 196616 | tf_op jit(solution)/shard_map/ppermute | solution.py:405
  59.8 6.6 %collective-permute-start.25 = (bf16[512,256]{1,0:T(8,128)(2,1)S(1)}, bf16[512,256]{1,0:T(8,128)(2,1)S(1)}, u32[]{:S(2)}, u32[]{:S(2)}) collective-permute-start(bf16[512,256]{1,0:T(8,128)(2,1)S(1)} %get-tuple-element.76.refs_7_), channel_id=1, source_target_pairs={{0,2},{1,3},{2,4},{3,5},{4,6},{5,7},{6,0},{7,1},{8,10},{9,11},{10,... | collective-permute-start | bytes 786440 | tf_op jit(solution)/shard_map/ppermute | solution.py:384
  67.7 4.8 %collective-permute-done.16.refs_3_ = bf16[128,256]{1,0:T(8,128)(2,1)S(1)} collective-permute-done((bf16[128,256]{1,0:T(8,128)(2,1)S(1)}, bf16[128,256]{1,0:T(8,128)(2,1)S(1)}, u32[]{:S(2)}, u32[]{:S(2)}) %collective-permute-start.16) | collective-permute-done | bytes 65568 | tf_op jit(solution)/shard_map/ppermute | solution.py:406
  72.6 5.3 %collective-permute-start.18 = (bf16[16,256]{1,0:T(8,128)(2,1)S(1)}, bf16[16,256]{1,0:T(8,128)(2,1)S(1)}, u32[]{:S(2)}, u32[]{:S(2)}) collective-permute-start(bf16[16,256]{1,0:T(8,128)(2,1)S(1)} %pad_maximum_fusion.1), channel_id=1, source_target_pairs={{1,0},{8,1},{3,2},{10,3},{5,4},{12,5},{7,6},{14,7},{9,8},{16,9},{1... | collective-permute-start | bytes 24584 | tf_op jit(solution)/shard_map/ppermute | solution.py:415
  79.8 4.0 %collective-permute-done.17.refs_4_ = bf16[16,256]{1,0:T(8,128)(2,1)S(1)} collective-permute-done((bf16[16,256]{1,0:T(8,128)(2,1)S(1)}, bf16[16,256]{1,0:T(8,128)(2,1)S(1)}, u32[]{:S(2)}, u32[]{:S(2)}) %collective-permute-start.17) | collective-permute-done | bytes 8224 | tf_op jit(solution)/shard_map/ppermute | solution.py:414
  86.0 3.4 %collective-permute-start.27 = (bf16[128,256]{1,0:T(8,128)(2,1)S(1)}, bf16[128,256]{1,0:T(8,128)(2,1)S(1)}, u32[]{:S(2)}, u32[]{:S(2)}) collective-permute-start(bf16[128,256]{1,0:T(8,128)(2,1)S(1)} %get-tuple-element.81), channel_id=1, source_target_pairs={{0,64},{64,128},{128,192},{1,65},{65,129},{129,193},{2,66},{66,130... | collective-permute-start | bytes 196616 | tf_op jit(solution)/shard_map/ppermute | solution.py:405
  89.5 4.1 %collective-permute-start.22 = (bf16[512,256]{1,0:T(8,128)(2,1)S(1)}, bf16[512,256]{1,0:T(8,128)(2,1)S(1)}, u32[]{:S(2)}, u32[]{:S(2)}) collective-permute-start(bf16[512,256]{1,0:T(8,128)(2,1)S(1)} %get-tuple-element.77.refs_1_), channel_id=1, source_target_pairs={{2,0},{3,1},{4,2},{5,3},{6,4},{7,5},{0,6},{1,7},{10,8},{11,9},{12,... | collective-permute-start | bytes 786440 | tf_op jit(solution)/shard_map/ppermute | solution.py:387
  95.0 4.8 %collective-permute-done.28.refs_3_ = bf16[128,256]{1,0:T(8,128)(2,1)S(1)} collective-permute-done((bf16[128,256]{1,0:T(8,128)(2,1)S(1)}, bf16[128,256]{1,0:T(8,128)(2,1)S(1)}, u32[]{:S(2)}, u32[]{:S(2)}) %collective-permute-start.28) | collective-permute-done | bytes 65568 | tf_op jit(solution)/shard_map/ppermute | solution.py:406
  105.7 4.2 %collective-permute-start.24 = (bf16[256,256]{1,0:T(8,128)(2,1)S(1)}, bf16[256,256]{1,0:T(8,128)(2,1)S(1)}, u32[]{:S(2)}, u32[]{:S(2)}) collective-permute-start(bf16[256,256]{1,0:T(8,128)(2,1)S(1)} %slice.87), channel_id=1, source_target_pairs={{2,0},{3,1},{4,2},{5,3},{6,4},{7,5},{0,6},{1,7},{10,8},{11,9},{12,... | collective-permute-start | bytes 393224 | tf_op jit(solution)/shard_map/ppermute | solution.py:387
  109.9 3.7 %back_kernel.1 = (bf16[512,256]{1,0:T(8,128)(2,1)S(1)}, f32[1024,256]{1,0:T(8,128)S(1)}, bf16[1024,256]{1,0:T(8,128)(2,1)S(1)}, bf16[512,256]{1,0:T(8,128)(2,1)S...) custom-call(s32[3]{0:T(128)S(1)} %pad_add_fusion.refs_0_, ...), custom_call_target="tpu_custom_call" | custom-call | flops 30000001024 | bytes 30000001024 | tf_op jit(solution)/shard_map/back_kernel/pallas_call | solution.py:24
  115.0 2.7 %collective-permute-start.37 = (bf16[1168,256]{1,0:T(8,128)(2,1)S(1)}, bf16[1168,256]{1,0:T(8,128)(2,1)S(1)}, u32[]{:S(2)}, u32[]{:S(2)}) collective-permute-start(bf16[1168,256]{1,0:T(8,128)(2,1)S(1)} %get-tuple-element.104), channel_id=1, source_target_pairs={{0,1},{1,0},{2,3},{3,2},{4,5},{5,4},{6,7},{7,6},{8,9},{9,8},{10,11... | collective-permute-start | bytes 1794056 | tf_op jit(solution)/shard_map/ppermute | solution.py:381
  120.3 3.7 %collective-permute-start.33 = (bf16[512,256]{1,0:T(8,128)(2,1)S(1)}, bf16[512,256]{1,0:T(8,128)(2,1)S(1)}, u32[]{:S(2)}, u32[]{:S(2)}) collective-permute-start(bf16[512,256]{1,0:T(8,128)(2,1)S(1)} %get-tuple-element.94), channel_id=1, source_target_pairs={{2,0},{3,1},{4,2},{5,3},{6,4},{7,5},{0,6},{1,7},{10,8},{11,9},{12,... | collective-permute-start | bytes 786440 | tf_op jit(solution)/shard_map/ppermute | solution.py:387
  129.6 5.7 %collective-permute-done.32.refs_3_ = bf16[512,256]{1,0:T(8,128)(2,1)S(1)} collective-permute-done((bf16[512,256]{1,0:T(8,128)(2,1)S(1)}, bf16[512,256]{1,0:T(8,128)(2,1)S(1)}, u32[]{:S(2)}, u32[]{:S(2)}) %collective-permute-start.32) | collective-permute-done | bytes 262176 | tf_op jit(solution)/shard_map/ppermute | solution.py:384
  136.0 3.5 %collective-permute-start.34 = (bf16[1024,256]{1,0:T(8,128)(2,1)S(1)}, bf16[1024,256]{1,0:T(8,128)(2,1)S(1)}, u32[]{:S(2)}, u32[]{:S(2)}) collective-permute-start(bf16[1024,256]{1,0:T(8,128)(2,1)S(1)} %get-tuple-element.100), channel_id=1, source_target_pairs={{0,2},{1,3},{2,4},{3,5},{4,6},{5,7},{6,0},{7,1},{8,10},{9,11},{10,... | collective-permute-start | bytes 1572872 | tf_op jit(solution)/shard_map/ppermute | solution.py:384
  140.3 2.7 %collective-permute-done.40.refs_3_ = bf16[656,256]{1,0:T(8,128)(2,1)S(1)} collective-permute-done((bf16[656,256]{1,0:T(8,128)(2,1)S(1)}, bf16[656,256]{1,0:T(8,128)(2,1)S(1)}, u32[]{:S(2)}, u32[]{:S(2)}) %collective-permute-start.40) | collective-permute-done | bytes 335904 | tf_op jit(solution)/shard_map/ppermute | solution.py:391
  143.0 2.7 %collective-permute-done.41.refs_4_ = bf16[656,256]{1,0:T(8,128)(2,1)S(1)} collective-permute-done((bf16[656,256]{1,0:T(8,128)(2,1)S(1)}, bf16[656,256]{1,0:T(8,128)(2,1)S(1)}, u32[]{:S(2)}, u32[]{:S(2)}) %collective-permute-start.41) | collective-permute-done | bytes 335904 | tf_op jit(solution)/shard_map/ppermute | solution.py:391
  147.8 3.3 %collective-permute-start.44 = (bf16[656,256]{1,0:T(8,128)(2,1)S(1)}, bf16[656,256]{1,0:T(8,128)(2,1)S(1)}, u32[]{:S(2)}, u32[]{:S(2)}) collective-permute-start(bf16[656,256]{1,0:T(8,128)(2,1)S(1)} %sum_y_kernel.1.refs_1_), channel_id=1, source_target_pairs={{0,192},{64,128},{128,64},{192,0},{1,193},{65,129},{129,65},{193,1... | collective-permute-start | bytes 1007624 | tf_op jit(solution)/shard_map/ppermute | solution.py:516
  151.2 8.7 %collective-permute-done.34.refs_2_ = bf16[1024,256]{1,0:T(8,128)(2,1)S(1)} collective-permute-done((bf16[1024,256]{1,0:T(8,128)(2,1)S(1)}, bf16[1024,256]{1,0:T(8,128)(2,1)S(1)}, u32[]{:S(2)}, u32[]{:S(2)}) %collective-permute-start.34) | collective-permute-done | bytes 524320 | tf_op jit(solution)/shard_map/ppermute | solution.py:384
  (124 shorter events, 62.0 us)
Async XLA Ops:
  10.6 28.2 %collective-permute-start.3 = (bf16[2,512,256]{2,1,0:T(8,128)(2,1)S(1)}, bf16[2,512,256]{2,1,0:T(8,128)(2,1)S(1)}, u32[]{:S(2)}, u32[]{:S(2)}) collective-permute-start(bf16[2,512,256]{2,1,0:T(8,128)(2,1)S(1)} %get-tuple-element.62.refs_5_.refs_1_.refs_8_), channel_id=1, source_target_pairs={{0,2},{1,3},{2,4},{3,5},{4,6},{5,7},{6,0},{7,1},{8,10},{9,11},{10,... | collective-permute-start | bytes 1572872 | tf_op jit(solution)/shard_map/ppermute | solution.py:384
  13.6 26.3 %collective-permute-start.4 = (bf16[2,512,256]{2,1,0:T(8,128)(2,1)S(1)}, bf16[2,512,256]{2,1,0:T(8,128)(2,1)S(1)}, u32[]{:S(2)}, u32[]{:S(2)}) collective-permute-start(bf16[2,512,256]{2,1,0:T(8,128)(2,1)S(1)} %get-tuple-element.62.refs_5_.refs_1_.refs_8_), channel_id=1, source_target_pairs={{2,0},{3,1},{4,2},{5,3},{6,4},{7,5},{0,6},{1,7},{10,8},{11,9},{12,... | collective-permute-start | bytes 1572872 | tf_op jit(solution)/shard_map/ppermute | solution.py:387
  16.4 22.3 %collective-permute-start.7 = (bf16[2,512,128]{2,1,0:T(8,128)(2,1)S(1)}, bf16[2,512,128]{2,1,0:T(8,128)(2,1)S(1)}, u32[]{:S(2)}, u32[]{:S(2)}) collective-permute-start(bf16[2,512,128]{2,1,0:T(8,128)(2,1)S(1)} %panel_kernel.1.refs_1_), channel_id=1, source_target_pairs={{0,16},{8,24},{16,0},{24,8},{32,48},{40,56},{48,32},{56,40},{1,17}... | collective-permute-start | bytes 786440 | tf_op jit(solution)/shard_map/ppermute | solution.py:391
  18.1 21.3 %collective-permute-start.8 = (bf16[2,512,128]{2,1,0:T(8,128)(2,1)S(1)}, bf16[2,512,128]{2,1,0:T(8,128)(2,1)S(1)}, u32[]{:S(2)}, u32[]{:S(2)}) collective-permute-start(bf16[2,512,128]{2,1,0:T(8,128)(2,1)S(1)} %panel_kernel.1.refs_1_), channel_id=1, source_target_pairs={{0,32},{8,40},{16,48},{24,56},{32,0},{40,8},{48,16},{56,24},{1,33}... | collective-permute-start | bytes 786440 | tf_op jit(solution)/shard_map/ppermute | solution.py:391
  21.0 18.5 %collective-permute-start.9 = (bf16[2,512,128]{2,1,0:T(8,128)(2,1)S(1)}, bf16[2,512,128]{2,1,0:T(8,128)(2,1)S(1)}, u32[]{:S(2)}, u32[]{:S(2)}) collective-permute-start(bf16[2,512,128]{2,1,0:T(8,128)(2,1)S(1)} %panel_kernel.1.refs_1_), channel_id=1, source_target_pairs={{0,48},{8,56},{16,32},{24,40},{32,16},{40,24},{48,0},{56,8},{1,49}... | collective-permute-start | bytes 786440 | tf_op jit(solution)/shard_map/ppermute | solution.py:391
  40.4 13.7 %collective-permute-start.5 = (bf16[512,256]{1,0:T(8,128)(2,1)S(1)}, bf16[512,256]{1,0:T(8,128)(2,1)S(1)}, u32[]{:S(2)}, u32[]{:S(2)}) collective-permute-start(bf16[512,256]{1,0:T(8,128)(2,1)S(1)} %slice_bitcast_fusion.1), channel_id=1, source_target_pairs={{0,2},{1,3},{2,4},{3,5},{4,6},{5,7},{6,0},{7,1},{8,10},{9,11},{10,... | collective-permute-start | bytes 786440 | tf_op jit(solution)/shard_map/ppermute | solution.py:384
  46.9 12.2 %collective-permute-start.19 = (bf16[256,256]{1,0:T(8,128)(2,1)S(1)}, bf16[256,256]{1,0:T(8,128)(2,1)S(1)}, u32[]{:S(2)}, u32[]{:S(2)}) collective-permute-start(bf16[256,256]{1,0:T(8,128)(2,1)S(1)} %get-tuple-element.74), channel_id=1, source_target_pairs={{0,2},{1,3},{2,4},{3,5},{4,6},{5,7},{6,0},{7,1},{8,10},{9,11},{10,... | collective-permute-start | bytes 393224 | tf_op jit(solution)/shard_map/ppermute | solution.py:384
  55.7 12.0 %collective-permute-start.15 = (bf16[128,256]{1,0:T(8,128)(2,1)S(1)}, bf16[128,256]{1,0:T(8,128)(2,1)S(1)}, u32[]{:S(2)}, u32[]{:S(2)}) collective-permute-start(bf16[128,256]{1,0:T(8,128)(2,1)S(1)} %get-tuple-element.64), channel_id=1, source_target_pairs={{0,64},{64,128},{128,192},{1,65},{65,129},{129,193},{2,66},{66,130... | collective-permute-start | bytes 196616 | tf_op jit(solution)/shard_map/ppermute | solution.py:405
  59.8 25.4 %collective-permute-start.25 = (bf16[512,256]{1,0:T(8,128)(2,1)S(1)}, bf16[512,256]{1,0:T(8,128)(2,1)S(1)}, u32[]{:S(2)}, u32[]{:S(2)}) collective-permute-start(bf16[512,256]{1,0:T(8,128)(2,1)S(1)} %get-tuple-element.76.refs_7_), channel_id=1, source_target_pairs={{0,2},{1,3},{2,4},{3,5},{4,6},{5,7},{6,0},{7,1},{8,10},{9,11},{10,... | collective-permute-start | bytes 786440 | tf_op jit(solution)/shard_map/ppermute | solution.py:384
  66.3 18.8 %collective-permute-start.26 = (bf16[512,256]{1,0:T(8,128)(2,1)S(1)}, bf16[512,256]{1,0:T(8,128)(2,1)S(1)}, u32[]{:S(2)}, u32[]{:S(2)}) collective-permute-start(bf16[512,256]{1,0:T(8,128)(2,1)S(1)} %get-tuple-element.79), channel_id=1, source_target_pairs={{2,0},{3,1},{4,2},{5,3},{6,4},{7,5},{0,6},{1,7},{10,8},{11,9},{12,... | collective-permute-start | bytes 786440 | tf_op jit(solution)/shard_map/ppermute | solution.py:387
  89.4 16.2 %collective-permute-start.21 = (bf16[512,256]{1,0:T(8,128)(2,1)S(1)}, bf16[512,256]{1,0:T(8,128)(2,1)S(1)}, u32[]{:S(2)}, u32[]{:S(2)}) collective-permute-start(bf16[512,256]{1,0:T(8,128)(2,1)S(1)} %get-tuple-element.77.refs_1_), channel_id=1, source_target_pairs={{0,2},{1,3},{2,4},{3,5},{4,6},{5,7},{6,0},{7,1},{8,10},{9,11},{10,... | collective-permute-start | bytes 786440 | tf_op jit(solution)/shard_map/ppermute | solution.py:384
  89.5 16.2 %collective-permute-start.22 = (bf16[512,256]{1,0:T(8,128)(2,1)S(1)}, bf16[512,256]{1,0:T(8,128)(2,1)S(1)}, u32[]{:S(2)}, u32[]{:S(2)}) collective-permute-start(bf16[512,256]{1,0:T(8,128)(2,1)S(1)} %get-tuple-element.77.refs_1_), channel_id=1, source_target_pairs={{2,0},{3,1},{4,2},{5,3},{6,4},{7,5},{0,6},{1,7},{10,8},{11,9},{12,... | collective-permute-start | bytes 786440 | tf_op jit(solution)/shard_map/ppermute | solution.py:387
  105.6 12.1 %collective-permute-start.23 = (bf16[256,256]{1,0:T(8,128)(2,1)S(1)}, bf16[256,256]{1,0:T(8,128)(2,1)S(1)}, u32[]{:S(2)}, u32[]{:S(2)}) collective-permute-start(bf16[256,256]{1,0:T(8,128)(2,1)S(1)} %slice.86), channel_id=1, source_target_pairs={{0,2},{1,3},{2,4},{3,5},{4,6},{5,7},{6,0},{7,1},{8,10},{9,11},{10,... | collective-permute-start | bytes 393224 | tf_op jit(solution)/shard_map/ppermute | solution.py:384
  105.7 12.0 %collective-permute-start.24 = (bf16[256,256]{1,0:T(8,128)(2,1)S(1)}, bf16[256,256]{1,0:T(8,128)(2,1)S(1)}, u32[]{:S(2)}, u32[]{:S(2)}) collective-permute-start(bf16[256,256]{1,0:T(8,128)(2,1)S(1)} %slice.87), channel_id=1, source_target_pairs={{2,0},{3,1},{4,2},{5,3},{6,4},{7,5},{0,6},{1,7},{10,8},{11,9},{12,... | collective-permute-start | bytes 393224 | tf_op jit(solution)/shard_map/ppermute | solution.py:387
  119.9 15.5 %collective-permute-start.32 = (bf16[512,256]{1,0:T(8,128)(2,1)S(1)}, bf16[512,256]{1,0:T(8,128)(2,1)S(1)}, u32[]{:S(2)}, u32[]{:S(2)}) collective-permute-start(bf16[512,256]{1,0:T(8,128)(2,1)S(1)} %get-tuple-element.93), channel_id=1, source_target_pairs={{0,2},{1,3},{2,4},{3,5},{4,6},{5,7},{6,0},{7,1},{8,10},{9,11},{10,... | collective-permute-start | bytes 786440 | tf_op jit(solution)/shard_map/ppermute | solution.py:384
  120.3 15.0 %collective-permute-start.33 = (bf16[512,256]{1,0:T(8,128)(2,1)S(1)}, bf16[512,256]{1,0:T(8,128)(2,1)S(1)}, u32[]{:S(2)}, u32[]{:S(2)}) collective-permute-start(bf16[512,256]{1,0:T(8,128)(2,1)S(1)} %get-tuple-element.94), channel_id=1, source_target_pairs={{2,0},{3,1},{4,2},{5,3},{6,4},{7,5},{0,6},{1,7},{10,8},{11,9},{12,... | collective-permute-start | bytes 786440 | tf_op jit(solution)/shard_map/ppermute | solution.py:387
  124.8 15.5 %collective-permute-start.39 = (bf16[656,256]{1,0:T(8,128)(2,1)S(1)}, bf16[656,256]{1,0:T(8,128)(2,1)S(1)}, u32[]{:S(2)}, u32[]{:S(2)}) collective-permute-start(bf16[656,256]{1,0:T(8,128)(2,1)S(1)} %get-tuple-element.107), channel_id=1, source_target_pairs={{0,16},{8,24},{16,0},{24,8},{32,48},{40,56},{48,32},{56,40},{1,17}... | collective-permute-start | bytes 1007624 | tf_op jit(solution)/shard_map/ppermute | solution.py:391
  126.5 16.5 %collective-permute-start.40 = (bf16[656,256]{1,0:T(8,128)(2,1)S(1)}, bf16[656,256]{1,0:T(8,128)(2,1)S(1)}, u32[]{:S(2)}, u32[]{:S(2)}) collective-permute-start(bf16[656,256]{1,0:T(8,128)(2,1)S(1)} %get-tuple-element.108), channel_id=1, source_target_pairs={{0,32},{8,40},{16,48},{24,56},{32,0},{40,8},{48,16},{56,24},{1,33}... | collective-permute-start | bytes 1007624 | tf_op jit(solution)/shard_map/ppermute | solution.py:391
  127.9 17.8 %collective-permute-start.41 = (bf16[656,256]{1,0:T(8,128)(2,1)S(1)}, bf16[656,256]{1,0:T(8,128)(2,1)S(1)}, u32[]{:S(2)}, u32[]{:S(2)}) collective-permute-start(bf16[656,256]{1,0:T(8,128)(2,1)S(1)} %get-tuple-element.109), channel_id=1, source_target_pairs={{0,48},{8,56},{16,32},{24,40},{32,16},{40,24},{48,0},{56,8},{1,49}... | collective-permute-start | bytes 1007624 | tf_op jit(solution)/shard_map/ppermute | solution.py:391
  136.0 23.8 %collective-permute-start.34 = (bf16[1024,256]{1,0:T(8,128)(2,1)S(1)}, bf16[1024,256]{1,0:T(8,128)(2,1)S(1)}, u32[]{:S(2)}, u32[]{:S(2)}) collective-permute-start(bf16[1024,256]{1,0:T(8,128)(2,1)S(1)} %get-tuple-element.100), channel_id=1, source_target_pairs={{0,2},{1,3},{2,4},{3,5},{4,6},{5,7},{6,0},{7,1},{8,10},{9,11},{10,... | collective-permute-start | bytes 1572872 | tf_op jit(solution)/shard_map/ppermute | solution.py:384
  139.5 21.7 %collective-permute-start.35 = (bf16[1024,256]{1,0:T(8,128)(2,1)S(1)}, bf16[1024,256]{1,0:T(8,128)(2,1)S(1)}, u32[]{:S(2)}, u32[]{:S(2)}) collective-permute-start(bf16[1024,256]{1,0:T(8,128)(2,1)S(1)} %get-tuple-element.101), channel_id=1, source_target_pairs={{2,0},{3,1},{4,2},{5,3},{6,4},{7,5},{0,6},{1,7},{10,8},{11,9},{12,... | collective-permute-start | bytes 1572872 | tf_op jit(solution)/shard_map/ppermute | solution.py:387
  146.4 15.6 %collective-permute-start.42 = (bf16[656,256]{1,0:T(8,128)(2,1)S(1)}, bf16[656,256]{1,0:T(8,128)(2,1)S(1)}, u32[]{:S(2)}, u32[]{:S(2)}) collective-permute-start(bf16[656,256]{1,0:T(8,128)(2,1)S(1)} %sum_y_kernel.1.refs_1_), channel_id=1, source_target_pairs={{0,64},{64,0},{128,192},{192,128},{1,65},{65,1},{129,193},{193,129... | collective-permute-start | bytes 1007624 | tf_op jit(solution)/shard_map/ppermute | solution.py:516
  147.7 14.3 %collective-permute-start.43 = (bf16[656,256]{1,0:T(8,128)(2,1)S(1)}, bf16[656,256]{1,0:T(8,128)(2,1)S(1)}, u32[]{:S(2)}, u32[]{:S(2)}) collective-permute-start(bf16[656,256]{1,0:T(8,128)(2,1)S(1)} %sum_y_kernel.1.refs_1_), channel_id=1, source_target_pairs={{0,128},{64,192},{128,0},{192,64},{1,129},{65,193},{129,1},{193,65... | collective-permute-start | bytes 1007624 | tf_op jit(solution)/shard_map/ppermute | solution.py:516
  147.8 16.7 %collective-permute-start.44 = (bf16[656,256]{1,0:T(8,128)(2,1)S(1)}, bf16[656,256]{1,0:T(8,128)(2,1)S(1)}, u32[]{:S(2)}, u32[]{:S(2)}) collective-permute-start(bf16[656,256]{1,0:T(8,128)(2,1)S(1)} %sum_y_kernel.1.refs_1_), channel_id=1, source_target_pairs={{0,192},{64,128},{128,64},{192,0},{1,193},{65,129},{129,65},{193,1... | collective-permute-start | bytes 1007624 | tf_op jit(solution)/shard_map/ppermute | solution.py:516
  (29 other events, 242.6 us)

commit v4 on v3

--- a/solution.py
+++ b/solution.py
@@ -418,10 +418,10 @@
     taps = group_weight.reshape(-1, own_mid)
     beside = [lax.ppermute(w, "chan", xor("chan", 1)) for w in (first_weight, third_weight)]
 
-    own, send = call(split_kernel, [(pair, BF16)] * 2, (place, images, out_grad))
-    img, grad = call(
-        join_kernel, [(pair, BF16)] * 2, (place, own, swap(send)), after=beside
-    )
+    own, send = call(
+        split_kernel, [(pair, BF16)] * 2, (place, images, out_grad), after=beside
+    )
+    img, grad = call(join_kernel, [(pair, BF16)] * 2, (place, own, swap(send)))
     left, right = up_z(img), down_z(img)
     blocks = (img, left, right, up_z(left[0]), down_z(right[1]))
 

time: 174 us -> 178 us (1.023)
  waiting for transfers between devices: 64.8 us -> 73.1 us
  starting transfers between devices: 79.8 us -> 74.6 us
    ppermute x8, waiting for transfers between devices: 34.8 us -> 45 us  [up_z(): return lax.ppermute(v, 'filt', zplus)]
    ppermute x8, starting transfers between devices: 18.7 us -> 13.4 us  [up_z(): return lax.ppermute(v, 'filt', zplus)]
    ppermute x2, starting transfers between devices: 7.22 us -> 3.86 us  [halo(): high = lax.ppermute(line(first, 0), ('chan', 'filt'), col_prev)]
    ppermute x3, waiting for transfers between devices: 2.56 us -> 0.01 us  [body(): others = [lax.ppermute(total, 'rows', xor('rows', k)) for k in range(1, 4)]]
    ppermute x8, starting transfers between devices: 18.5 us -> 20.8 us  [down_z(): return lax.ppermute(v, 'filt', zminus)]
    ppermute x10, waiting for transfers between devices: 0.37 us -> 2.27 us  [swap(): return lax.ppermute(v, 'filt', xor('filt', 1))]
  transfers between devices with their start and end apart: 46 -> 46, of which waited for: 16 -> 15; matrix products, arithmetic and copies ran while one was open for 0% -> 0% of each run, Pallas kernels for 12% -> 12%
where the time goes in v4:
time: 178 us; the launch traced here: 176 us
  starting transfers between devices  74.6 us (42%)
  waiting for transfers between devices  73.1 us (41%)
  Pallas kernels  24.4 us (14%)
  local copies, waits for them, and re-layouts  2.23 us (1%)
    ppermute x8, waiting for transfers between devices, up_z(): return lax.ppermute(v, 'filt', zplus)  45 us
    pallas_call x21, Pallas kernels, call(): pl.pallas_call(ordered, out_shape=[jax.ShapeDtypeStruct(s, d) for s, d in...  24.4 us
    ppermute x8, starting transfers between devices, down_z(): return lax.ppermute(v, 'filt', zminus)  20.8 us
    ppermute x8, starting transfers between devices, up_z(): return lax.ppermute(v, 'filt', zplus)  13.4 us
    ppermute x2, waiting for transfers between devices, halo(): down = lax.ppermute(top, 'rows', row_prev)  9.67 us
    ppermute x6, starting transfers between devices, along_y(): lax.ppermute(pieces[k], 'chan', xor('chan', 2 * k))  9.57 us
    ppermute x2, starting transfers between devices, halo(): up = lax.ppermute(bottom, 'rows', row_next)  6.79 us
    ppermute x10, starting transfers between devices, swap(): return lax.ppermute(v, 'filt', xor('filt', 1))  4.93 us
  transfers between devices with their start and end apart: 46, of which 15 were waited for; matrix products, arithmetic and copies ran while one was open for 0% of the time, Pallas kernels for 12%

profile of v4, /device:TPU:32, one launch (start us, length us, event | category | flops | bytes accessed | tf_op | source)
XLA Modules:
  0.0 175.6 jit_solution(4597771891243999946)
XLA Ops:
  2.8 2.6 %collective-permute-done.refs_3_ = bf16[256,128]{1,0:T(8,128)(2,1)S(1)} collective-permute-done((bf16[256,128]{1,0:T(8,128)(2,1)}, bf16[256,128]{1,0:T(8,128)(2,1)S(1)}, u32[]{:S(2)}, u32[]{:S(2)}) %collective-permute-start) | collective-permute-done | bytes 65568 | tf_op jit(solution)/shard_map/ppermute | solution.py:419
  12.4 2.5 %collective-permute-start.3 = (bf16[2,512,256]{2,1,0:T(8,128)(2,1)S(1)}, bf16[2,512,256]{2,1,0:T(8,128)(2,1)S(1)}, u32[]{:S(2)}, u32[]{:S(2)}) collective-permute-start(bf16[2,512,256]{2,1,0:T(8,128)(2,1)S(1)} %get-tuple-element.62.refs_5_.refs_1_.refs_8_), channel_id=1, source_target_pairs={{0,2},{1,3},{2,4},{3,5},{4,6},{5,7},{6,0},{7,1},{8,10},{9,11},{10,... | collective-permute-start | bytes 1572872 | tf_op jit(solution)/shard_map/ppermute | solution.py:384
  19.3 2.9 %collective-permute-start.8 = (bf16[2,512,128]{2,1,0:T(8,128)(2,1)S(1)}, bf16[2,512,128]{2,1,0:T(8,128)(2,1)S(1)}, u32[]{:S(2)}, u32[]{:S(2)}) collective-permute-start(bf16[2,512,128]{2,1,0:T(8,128)(2,1)S(1)} %panel_kernel.1.refs_1_), channel_id=1, source_target_pairs={{0,32},{8,40},{16,48},{24,56},{32,0},{40,8},{48,16},{56,24},{1,33}... | collective-permute-start | bytes 786440 | tf_op jit(solution)/shard_map/ppermute | solution.py:391
  22.5 18.0 %collective-permute-done.3.refs_2_ = bf16[2,512,256]{2,1,0:T(8,128)(2,1)S(1)} collective-permute-done((bf16[2,512,256]{2,1,0:T(8,128)(2,1)S(1)}, bf16[2,512,256]{2,1,0:T(8,128)(2,1)S(1)}, u32[]{:S(2)}, u32[]{:S(2)}) %collective-permute-start.3) | collective-permute-done | bytes 524320 | tf_op jit(solution)/shard_map/ppermute | solution.py:384
  42.1 3.1 %collective-permute-start.5 = (bf16[512,256]{1,0:T(8,128)(2,1)S(1)}, bf16[512,256]{1,0:T(8,128)(2,1)S(1)}, u32[]{:S(2)}, u32[]{:S(2)}) collective-permute-start(bf16[512,256]{1,0:T(8,128)(2,1)S(1)} %slice_bitcast_fusion.1), channel_id=1, source_target_pairs={{0,2},{1,3},{2,4},{3,5},{4,6},{5,7},{6,0},{7,1},{8,10},{9,11},{10,... | collective-permute-start | bytes 786440 | tf_op jit(solution)/shard_map/ppermute | solution.py:384
  52.9 8.6 %collective-permute-done.5.refs_4_ = bf16[512,256]{1,0:T(8,128)(2,1)S(1)} collective-permute-done((bf16[512,256]{1,0:T(8,128)(2,1)S(1)}, bf16[512,256]{1,0:T(8,128)(2,1)S(1)}, u32[]{:S(2)}, u32[]{:S(2)}) %collective-permute-start.5) | collective-permute-done | bytes 262176 | tf_op jit(solution)/shard_map/ppermute | solution.py:384
  62.8 3.4 %collective-permute-start.15 = (bf16[128,256]{1,0:T(8,128)(2,1)S(1)}, bf16[128,256]{1,0:T(8,128)(2,1)S(1)}, u32[]{:S(2)}, u32[]{:S(2)}) collective-permute-start(bf16[128,256]{1,0:T(8,128)(2,1)S(1)} %get-tuple-element.64), channel_id=1, source_target_pairs={{0,64},{64,128},{128,192},{1,65},{65,129},{129,193},{2,66},{66,130... | collective-permute-start | bytes 196616 | tf_op jit(solution)/shard_map/ppermute | solution.py:405
  72.4 4.8 %collective-permute-done.16.refs_3_ = bf16[128,256]{1,0:T(8,128)(2,1)S(1)} collective-permute-done((bf16[128,256]{1,0:T(8,128)(2,1)S(1)}, bf16[128,256]{1,0:T(8,128)(2,1)S(1)}, u32[]{:S(2)}, u32[]{:S(2)}) %collective-permute-start.16) | collective-permute-done | bytes 65568 | tf_op jit(solution)/shard_map/ppermute | solution.py:406
  79.3 2.4 %collective-permute-start.17 = (bf16[16,256]{1,0:T(8,128)(2,1)S(1)}, bf16[16,256]{1,0:T(8,128)(2,1)S(1)}, u32[]{:S(2)}, u32[]{:S(2)}) collective-permute-start(bf16[16,256]{1,0:T(8,128)(2,1)S(1)} %pad_maximum_fusion), channel_id=1, source_target_pairs={{0,1},{1,8},{2,3},{3,10},{4,5},{5,12},{6,7},{7,14},{8,9},{9,16},{1... | collective-permute-start | bytes 24584 | tf_op jit(solution)/shard_map/ppermute | solution.py:414
  81.7 3.9 %collective-permute-done.17.refs_4_ = bf16[16,256]{1,0:T(8,128)(2,1)S(1)} collective-permute-done((bf16[16,256]{1,0:T(8,128)(2,1)S(1)}, bf16[16,256]{1,0:T(8,128)(2,1)S(1)}, u32[]{:S(2)}, u32[]{:S(2)}) %collective-permute-start.17) | collective-permute-done | bytes 8224 | tf_op jit(solution)/shard_map/ppermute | solution.py:414
  87.8 3.4 %collective-permute-start.27 = (bf16[128,256]{1,0:T(8,128)(2,1)S(1)}, bf16[128,256]{1,0:T(8,128)(2,1)S(1)}, u32[]{:S(2)}, u32[]{:S(2)}) collective-permute-start(bf16[128,256]{1,0:T(8,128)(2,1)S(1)} %get-tuple-element.81), channel_id=1, source_target_pairs={{0,64},{64,128},{128,192},{1,65},{65,129},{129,193},{2,66},{66,130... | collective-permute-start | bytes 196616 | tf_op jit(solution)/shard_map/ppermute | solution.py:405
  91.9 3.5 %collective-permute-start.22 = (bf16[512,256]{1,0:T(8,128)(2,1)S(1)}, bf16[512,256]{1,0:T(8,128)(2,1)S(1)}, u32[]{:S(2)}, u32[]{:S(2)}) collective-permute-start(bf16[512,256]{1,0:T(8,128)(2,1)S(1)} %get-tuple-element.77.refs_1_), channel_id=1, source_target_pairs={{2,0},{3,1},{4,2},{5,3},{6,4},{7,5},{0,6},{1,7},{10,8},{11,9},{12,... | collective-permute-start | bytes 786440 | tf_op jit(solution)/shard_map/ppermute | solution.py:387
  96.8 4.8 %collective-permute-done.28.refs_3_ = bf16[128,256]{1,0:T(8,128)(2,1)S(1)} collective-permute-done((bf16[128,256]{1,0:T(8,128)(2,1)S(1)}, bf16[128,256]{1,0:T(8,128)(2,1)S(1)}, u32[]{:S(2)}, u32[]{:S(2)}) %collective-permute-start.28) | collective-permute-done | bytes 65568 | tf_op jit(solution)/shard_map/ppermute | solution.py:406
  103.6 2.4 %collective-permute-start.29 = (bf16[16,256]{1,0:T(8,128)(2,1)S(1)}, bf16[16,256]{1,0:T(8,128)(2,1)S(1)}, u32[]{:S(2)}, u32[]{:S(2)}) collective-permute-start(bf16[16,256]{1,0:T(8,128)(2,1)S(1)} %pad_maximum_fusion.2), channel_id=1, source_target_pairs={{0,1},{1,8},{2,3},{3,10},{4,5},{5,12},{6,7},{7,14},{8,9},{9,16},{1... | collective-permute-start | bytes 24584 | tf_op jit(solution)/shard_map/ppermute | solution.py:414
  107.5 4.2 %collective-permute-start.24 = (bf16[256,256]{1,0:T(8,128)(2,1)S(1)}, bf16[256,256]{1,0:T(8,128)(2,1)S(1)}, u32[]{:S(2)}, u32[]{:S(2)}) collective-permute-start(bf16[256,256]{1,0:T(8,128)(2,1)S(1)} %slice.87), channel_id=1, source_target_pairs={{2,0},{3,1},{4,2},{5,3},{6,4},{7,5},{0,6},{1,7},{10,8},{11,9},{12,... | collective-permute-start | bytes 393224 | tf_op jit(solution)/shard_map/ppermute | solution.py:387
  111.7 3.7 %back_kernel.1 = (bf16[512,256]{1,0:T(8,128)(2,1)S(1)}, f32[1024,256]{1,0:T(8,128)S(1)}, bf16[1024,256]{1,0:T(8,128)(2,1)S(1)}, bf16[512,256]{1,0:T(8,128)(2,1)S...) custom-call(s32[3]{0:T(128)S(1)} %pad_add_fusion.refs_0_, ...), custom_call_target="tpu_custom_call" | custom-call | flops 30000001024 | bytes 30000001024 | tf_op jit(solution)/shard_map/back_kernel/pallas_call | solution.py:24
  116.8 2.7 %collective-permute-start.37 = (bf16[1168,256]{1,0:T(8,128)(2,1)S(1)}, bf16[1168,256]{1,0:T(8,128)(2,1)S(1)}, u32[]{:S(2)}, u32[]{:S(2)}) collective-permute-start(bf16[1168,256]{1,0:T(8,128)(2,1)S(1)} %get-tuple-element.104), channel_id=1, source_target_pairs={{0,1},{1,0},{2,3},{3,2},{4,5},{5,4},{6,7},{7,6},{8,9},{9,8},{10,11... | collective-permute-start | bytes 1794056 | tf_op jit(solution)/shard_map/ppermute | solution.py:381
  123.0 2.8 %collective-permute-start.33 = (bf16[512,256]{1,0:T(8,128)(2,1)S(1)}, bf16[512,256]{1,0:T(8,128)(2,1)S(1)}, u32[]{:S(2)}, u32[]{:S(2)}) collective-permute-start(bf16[512,256]{1,0:T(8,128)(2,1)S(1)} %get-tuple-element.94), channel_id=1, source_target_pairs={{2,0},{3,1},{4,2},{5,3},{6,4},{7,5},{0,6},{1,7},{10,8},{11,9},{12,... | collective-permute-start | bytes 786440 | tf_op jit(solution)/shard_map/ppermute | solution.py:387
  131.4 6.3 %collective-permute-done.32.refs_3_ = bf16[512,256]{1,0:T(8,128)(2,1)S(1)} collective-permute-done((bf16[512,256]{1,0:T(8,128)(2,1)S(1)}, bf16[512,256]{1,0:T(8,128)(2,1)S(1)}, u32[]{:S(2)}, u32[]{:S(2)}) %collective-permute-start.32) | collective-permute-done | bytes 262176 | tf_op jit(solution)/shard_map/ppermute | solution.py:384
  140.1 2.7 %collective-permute-start.35 = (bf16[1024,256]{1,0:T(8,128)(2,1)S(1)}, bf16[1024,256]{1,0:T(8,128)(2,1)S(1)}, u32[]{:S(2)}, u32[]{:S(2)}) collective-permute-start(bf16[1024,256]{1,0:T(8,128)(2,1)S(1)} %get-tuple-element.101), channel_id=1, source_target_pairs={{2,0},{3,1},{4,2},{5,3},{6,4},{7,5},{0,6},{1,7},{10,8},{11,9},{12,... | collective-permute-start | bytes 1572872 | tf_op jit(solution)/shard_map/ppermute | solution.py:387
  144.8 2.7 %collective-permute-done.41.refs_4_ = bf16[656,256]{1,0:T(8,128)(2,1)S(1)} collective-permute-done((bf16[656,256]{1,0:T(8,128)(2,1)S(1)}, bf16[656,256]{1,0:T(8,128)(2,1)S(1)}, u32[]{:S(2)}, u32[]{:S(2)}) %collective-permute-start.41) | collective-permute-done | bytes 335904 | tf_op jit(solution)/shard_map/ppermute | solution.py:391
  149.6 3.3 %collective-permute-start.44 = (bf16[656,256]{1,0:T(8,128)(2,1)S(1)}, bf16[656,256]{1,0:T(8,128)(2,1)S(1)}, u32[]{:S(2)}, u32[]{:S(2)}) collective-permute-start(bf16[656,256]{1,0:T(8,128)(2,1)S(1)} %sum_y_kernel.1.refs_1_), channel_id=1, source_target_pairs={{0,192},{64,128},{128,64},{192,0},{1,193},{65,129},{129,65},{193,1... | collective-permute-start | bytes 1007624 | tf_op jit(solution)/shard_map/ppermute | solution.py:516
  152.9 12.1 %collective-permute-done.34.refs_2_ = bf16[1024,256]{1,0:T(8,128)(2,1)S(1)} collective-permute-done((bf16[1024,256]{1,0:T(8,128)(2,1)S(1)}, bf16[1024,256]{1,0:T(8,128)(2,1)S(1)}, u32[]{:S(2)}, u32[]{:S(2)}) %collective-permute-start.34) | collective-permute-done | bytes 524320 | tf_op jit(solution)/shard_map/ppermute | solution.py:384
  171.1 3.1 %collective-permute-done.45.refs_3_ = bf16[400,256]{1,0:T(8,128)(2,1)S(1)} collective-permute-done((bf16[400,256]{1,0:T(8,128)(2,1)S(1)}, bf16[400,256]{1,0:T(8,128)(2,1)S(1)}, u32[]{:S(2)}, u32[]{:S(2)}) %collective-permute-start.45) | collective-permute-done | bytes 204832 | tf_op jit(solution)/shard_map/ppermute | solution.py:525
  (124 shorter events, 64.6 us)
Async XLA Ops:
  12.4 28.1 %collective-permute-start.3 = (bf16[2,512,256]{2,1,0:T(8,128)(2,1)S(1)}, bf16[2,512,256]{2,1,0:T(8,128)(2,1)S(1)}, u32[]{:S(2)}, u32[]{:S(2)}) collective-permute-start(bf16[2,512,256]{2,1,0:T(8,128)(2,1)S(1)} %get-tuple-element.62.refs_5_.refs_1_.refs_8_), channel_id=1, source_target_pairs={{0,2},{1,3},{2,4},{3,5},{4,6},{5,7},{6,0},{7,1},{8,10},{9,11},{10,... | collective-permute-start | bytes 1572872 | tf_op jit(solution)/shard_map/ppermute | solution.py:384
  14.8 26.8 %collective-permute-start.4 = (bf16[2,512,256]{2,1,0:T(8,128)(2,1)S(1)}, bf16[2,512,256]{2,1,0:T(8,128)(2,1)S(1)}, u32[]{:S(2)}, u32[]{:S(2)}) collective-permute-start(bf16[2,512,256]{2,1,0:T(8,128)(2,1)S(1)} %get-tuple-element.62.refs_5_.refs_1_.refs_8_), channel_id=1, source_target_pairs={{2,0},{3,1},{4,2},{5,3},{6,4},{7,5},{0,6},{1,7},{10,8},{11,9},{12,... | collective-permute-start | bytes 1572872 | tf_op jit(solution)/shard_map/ppermute | solution.py:387
  17.7 22.8 %collective-permute-start.7 = (bf16[2,512,128]{2,1,0:T(8,128)(2,1)S(1)}, bf16[2,512,128]{2,1,0:T(8,128)(2,1)S(1)}, u32[]{:S(2)}, u32[]{:S(2)}) collective-permute-start(bf16[2,512,128]{2,1,0:T(8,128)(2,1)S(1)} %panel_kernel.1.refs_1_), channel_id=1, source_target_pairs={{0,16},{8,24},{16,0},{24,8},{32,48},{40,56},{48,32},{56,40},{1,17}... | collective-permute-start | bytes 786440 | tf_op jit(solution)/shard_map/ppermute | solution.py:391
  19.3 21.8 %collective-permute-start.8 = (bf16[2,512,128]{2,1,0:T(8,128)(2,1)S(1)}, bf16[2,512,128]{2,1,0:T(8,128)(2,1)S(1)}, u32[]{:S(2)}, u32[]{:S(2)}) collective-permute-start(bf16[2,512,128]{2,1,0:T(8,128)(2,1)S(1)} %panel_kernel.1.refs_1_), channel_id=1, source_target_pairs={{0,32},{8,40},{16,48},{24,56},{32,0},{40,8},{48,16},{56,24},{1,33}... | collective-permute-start | bytes 786440 | tf_op jit(solution)/shard_map/ppermute | solution.py:391
  22.2 19.0 %collective-permute-start.9 = (bf16[2,512,128]{2,1,0:T(8,128)(2,1)S(1)}, bf16[2,512,128]{2,1,0:T(8,128)(2,1)S(1)}, u32[]{:S(2)}, u32[]{:S(2)}) collective-permute-start(bf16[2,512,128]{2,1,0:T(8,128)(2,1)S(1)} %panel_kernel.1.refs_1_), channel_id=1, source_target_pairs={{0,48},{8,56},{16,32},{24,40},{32,16},{40,24},{48,0},{56,8},{1,49}... | collective-permute-start | bytes 786440 | tf_op jit(solution)/shard_map/ppermute | solution.py:391
  42.1 19.4 %collective-permute-start.5 = (bf16[512,256]{1,0:T(8,128)(2,1)S(1)}, bf16[512,256]{1,0:T(8,128)(2,1)S(1)}, u32[]{:S(2)}, u32[]{:S(2)}) collective-permute-start(bf16[512,256]{1,0:T(8,128)(2,1)S(1)} %slice_bitcast_fusion.1), channel_id=1, source_target_pairs={{0,2},{1,3},{2,4},{3,5},{4,6},{5,7},{6,0},{7,1},{8,10},{9,11},{10,... | collective-permute-start | bytes 786440 | tf_op jit(solution)/shard_map/ppermute | solution.py:384
  45.2 16.4 %collective-permute-start.6 = (bf16[512,256]{1,0:T(8,128)(2,1)S(1)}, bf16[512,256]{1,0:T(8,128)(2,1)S(1)}, u32[]{:S(2)}, u32[]{:S(2)}) collective-permute-start(bf16[512,256]{1,0:T(8,128)(2,1)S(1)} %slice_bitcast_fusion), channel_id=1, source_target_pairs={{2,0},{3,1},{4,2},{5,3},{6,4},{7,5},{0,6},{1,7},{10,8},{11,9},{12,... | collective-permute-start | bytes 786440 | tf_op jit(solution)/shard_map/ppermute | solution.py:387
  48.7 17.5 %collective-permute-start.19 = (bf16[256,256]{1,0:T(8,128)(2,1)S(1)}, bf16[256,256]{1,0:T(8,128)(2,1)S(1)}, u32[]{:S(2)}, u32[]{:S(2)}) collective-permute-start(bf16[256,256]{1,0:T(8,128)(2,1)S(1)} %get-tuple-element.74), channel_id=1, source_target_pairs={{0,2},{1,3},{2,4},{3,5},{4,6},{5,7},{6,0},{7,1},{8,10},{9,11},{10,... | collective-permute-start | bytes 393224 | tf_op jit(solution)/shard_map/ppermute | solution.py:384
  50.6 15.6 %collective-permute-start.20 = (bf16[256,256]{1,0:T(8,128)(2,1)S(1)}, bf16[256,256]{1,0:T(8,128)(2,1)S(1)}, u32[]{:S(2)}, u32[]{:S(2)}) collective-permute-start(bf16[256,256]{1,0:T(8,128)(2,1)S(1)} %get-tuple-element.75), channel_id=1, source_target_pairs={{2,0},{3,1},{4,2},{5,3},{6,4},{7,5},{0,6},{1,7},{10,8},{11,9},{12,... | collective-permute-start | bytes 393224 | tf_op jit(solution)/shard_map/ppermute | solution.py:387
  66.9 20.1 %collective-permute-start.25 = (bf16[512,256]{1,0:T(8,128)(2,1)S(1)}, bf16[512,256]{1,0:T(8,128)(2,1)S(1)}, u32[]{:S(2)}, u32[]{:S(2)}) collective-permute-start(bf16[512,256]{1,0:T(8,128)(2,1)S(1)} %get-tuple-element.76.refs_7_), channel_id=1, source_target_pairs={{0,2},{1,3},{2,4},{3,5},{4,6},{5,7},{6,0},{7,1},{8,10},{9,11},{10,... | collective-permute-start | bytes 786440 | tf_op jit(solution)/shard_map/ppermute | solution.py:384
  69.1 17.9 %collective-permute-start.26 = (bf16[512,256]{1,0:T(8,128)(2,1)S(1)}, bf16[512,256]{1,0:T(8,128)(2,1)S(1)}, u32[]{:S(2)}, u32[]{:S(2)}) collective-permute-start(bf16[512,256]{1,0:T(8,128)(2,1)S(1)} %get-tuple-element.79), channel_id=1, source_target_pairs={{2,0},{3,1},{4,2},{5,3},{6,4},{7,5},{0,6},{1,7},{10,8},{11,9},{12,... | collective-permute-start | bytes 786440 | tf_op jit(solution)/shard_map/ppermute | solution.py:387
  91.2 16.2 %collective-permute-start.21 = (bf16[512,256]{1,0:T(8,128)(2,1)S(1)}, bf16[512,256]{1,0:T(8,128)(2,1)S(1)}, u32[]{:S(2)}, u32[]{:S(2)}) collective-permute-start(bf16[512,256]{1,0:T(8,128)(2,1)S(1)} %get-tuple-element.77.refs_1_), channel_id=1, source_target_pairs={{0,2},{1,3},{2,4},{3,5},{4,6},{5,7},{6,0},{7,1},{8,10},{9,11},{10,... | collective-permute-start | bytes 786440 | tf_op jit(solution)/shard_map/ppermute | solution.py:384
  91.9 15.6 %collective-permute-start.22 = (bf16[512,256]{1,0:T(8,128)(2,1)S(1)}, bf16[512,256]{1,0:T(8,128)(2,1)S(1)}, u32[]{:S(2)}, u32[]{:S(2)}) collective-permute-start(bf16[512,256]{1,0:T(8,128)(2,1)S(1)} %get-tuple-element.77.refs_1_), channel_id=1, source_target_pairs={{2,0},{3,1},{4,2},{5,3},{6,4},{7,5},{0,6},{1,7},{10,8},{11,9},{12,... | collective-permute-start | bytes 786440 | tf_op jit(solution)/shard_map/ppermute | solution.py:387
  107.4 12.1 %collective-permute-start.23 = (bf16[256,256]{1,0:T(8,128)(2,1)S(1)}, bf16[256,256]{1,0:T(8,128)(2,1)S(1)}, u32[]{:S(2)}, u32[]{:S(2)}) collective-permute-start(bf16[256,256]{1,0:T(8,128)(2,1)S(1)} %slice.86), channel_id=1, source_target_pairs={{0,2},{1,3},{2,4},{3,5},{4,6},{5,7},{6,0},{7,1},{8,10},{9,11},{10,... | collective-permute-start | bytes 393224 | tf_op jit(solution)/shard_map/ppermute | solution.py:384
  121.6 16.0 %collective-permute-start.32 = (bf16[512,256]{1,0:T(8,128)(2,1)S(1)}, bf16[512,256]{1,0:T(8,128)(2,1)S(1)}, u32[]{:S(2)}, u32[]{:S(2)}) collective-permute-start(bf16[512,256]{1,0:T(8,128)(2,1)S(1)} %get-tuple-element.93), channel_id=1, source_target_pairs={{0,2},{1,3},{2,4},{3,5},{4,6},{5,7},{6,0},{7,1},{8,10},{9,11},{10,... | collective-permute-start | bytes 786440 | tf_op jit(solution)/shard_map/ppermute | solution.py:384
  123.0 14.8 %collective-permute-start.33 = (bf16[512,256]{1,0:T(8,128)(2,1)S(1)}, bf16[512,256]{1,0:T(8,128)(2,1)S(1)}, u32[]{:S(2)}, u32[]{:S(2)}) collective-permute-start(bf16[512,256]{1,0:T(8,128)(2,1)S(1)} %get-tuple-element.94), channel_id=1, source_target_pairs={{2,0},{3,1},{4,2},{5,3},{6,4},{7,5},{0,6},{1,7},{10,8},{11,9},{12,... | collective-permute-start | bytes 786440 | tf_op jit(solution)/shard_map/ppermute | solution.py:387
  126.6 16.2 %collective-permute-start.39 = (bf16[656,256]{1,0:T(8,128)(2,1)S(1)}, bf16[656,256]{1,0:T(8,128)(2,1)S(1)}, u32[]{:S(2)}, u32[]{:S(2)}) collective-permute-start(bf16[656,256]{1,0:T(8,128)(2,1)S(1)} %get-tuple-element.107), channel_id=1, source_target_pairs={{0,16},{8,24},{16,0},{24,8},{32,48},{40,56},{48,32},{56,40},{1,17}... | collective-permute-start | bytes 1007624 | tf_op jit(solution)/shard_map/ppermute | solution.py:391
  128.2 16.5 %collective-permute-start.40 = (bf16[656,256]{1,0:T(8,128)(2,1)S(1)}, bf16[656,256]{1,0:T(8,128)(2,1)S(1)}, u32[]{:S(2)}, u32[]{:S(2)}) collective-permute-start(bf16[656,256]{1,0:T(8,128)(2,1)S(1)} %get-tuple-element.108), channel_id=1, source_target_pairs={{0,32},{8,40},{16,48},{24,56},{32,0},{40,8},{48,16},{56,24},{1,33}... | collective-permute-start | bytes 1007624 | tf_op jit(solution)/shard_map/ppermute | solution.py:391
  129.7 17.8 %collective-permute-start.41 = (bf16[656,256]{1,0:T(8,128)(2,1)S(1)}, bf16[656,256]{1,0:T(8,128)(2,1)S(1)}, u32[]{:S(2)}, u32[]{:S(2)}) collective-permute-start(bf16[656,256]{1,0:T(8,128)(2,1)S(1)} %get-tuple-element.109), channel_id=1, source_target_pairs={{0,48},{8,56},{16,32},{24,40},{32,16},{40,24},{48,0},{56,8},{1,49}... | collective-permute-start | bytes 1007624 | tf_op jit(solution)/shard_map/ppermute | solution.py:391
  138.5 26.5 %collective-permute-start.34 = (bf16[1024,256]{1,0:T(8,128)(2,1)S(1)}, bf16[1024,256]{1,0:T(8,128)(2,1)S(1)}, u32[]{:S(2)}, u32[]{:S(2)}) collective-permute-start(bf16[1024,256]{1,0:T(8,128)(2,1)S(1)} %get-tuple-element.100), channel_id=1, source_target_pairs={{0,2},{1,3},{2,4},{3,5},{4,6},{5,7},{6,0},{7,1},{8,10},{9,11},{10,... | collective-permute-start | bytes 1572872 | tf_op jit(solution)/shard_map/ppermute | solution.py:384
  140.1 25.0 %collective-permute-start.35 = (bf16[1024,256]{1,0:T(8,128)(2,1)S(1)}, bf16[1024,256]{1,0:T(8,128)(2,1)S(1)}, u32[]{:S(2)}, u32[]{:S(2)}) collective-permute-start(bf16[1024,256]{1,0:T(8,128)(2,1)S(1)} %get-tuple-element.101), channel_id=1, source_target_pairs={{2,0},{3,1},{4,2},{5,3},{6,4},{7,5},{0,6},{1,7},{10,8},{11,9},{12,... | collective-permute-start | bytes 1572872 | tf_op jit(solution)/shard_map/ppermute | solution.py:387
  148.2 18.3 %collective-permute-start.42 = (bf16[656,256]{1,0:T(8,128)(2,1)S(1)}, bf16[656,256]{1,0:T(8,128)(2,1)S(1)}, u32[]{:S(2)}, u32[]{:S(2)}) collective-permute-start(bf16[656,256]{1,0:T(8,128)(2,1)S(1)} %sum_y_kernel.1.refs_1_), channel_id=1, source_target_pairs={{0,64},{64,0},{128,192},{192,128},{1,65},{65,1},{129,193},{193,129... | collective-permute-start | bytes 1007624 | tf_op jit(solution)/shard_map/ppermute | solution.py:516
  149.4 17.0 %collective-permute-start.43 = (bf16[656,256]{1,0:T(8,128)(2,1)S(1)}, bf16[656,256]{1,0:T(8,128)(2,1)S(1)}, u32[]{:S(2)}, u32[]{:S(2)}) collective-permute-start(bf16[656,256]{1,0:T(8,128)(2,1)S(1)} %sum_y_kernel.1.refs_1_), channel_id=1, source_target_pairs={{0,128},{64,192},{128,0},{192,64},{1,129},{65,193},{129,1},{193,65... | collective-permute-start | bytes 1007624 | tf_op jit(solution)/shard_map/ppermute | solution.py:516
  149.6 16.8 %collective-permute-start.44 = (bf16[656,256]{1,0:T(8,128)(2,1)S(1)}, bf16[656,256]{1,0:T(8,128)(2,1)S(1)}, u32[]{:S(2)}, u32[]{:S(2)}) collective-permute-start(bf16[656,256]{1,0:T(8,128)(2,1)S(1)} %sum_y_kernel.1.refs_1_), channel_id=1, source_target_pairs={{0,192},{64,128},{128,64},{192,0},{1,193},{65,129},{129,65},{193,1... | collective-permute-start | bytes 1007624 | tf_op jit(solution)/shard_map/ppermute | solution.py:516
  (29 other events, 220.3 us)
